TPU v7x, 256 devices: a whole 4x4x8 slice. The times are simulated.
256 devices in a mesh: band: 32 (over z_hi, x, core), grid: 8 (over y, z_lo).
Axes of the slice: x: 4, y: 4, z: 8 (z_hi: 4, z_lo: 2; z = z_hi * 2 + z_lo), core: 2. Of those that a mesh axis runs over, the one named last changes fastest.
Arguments:
- orbitals: bfloat16 [64, 192, 36864], P('band', 'grid'), may hold values from -6 to 6
Outputs:
- exchange_applied: float32 [32, 192, 36864], P('band', 'grid')
All inputs are finite; a program needn't handle non-finite values.
Results may differ from a plain program's by a relative error of at most 0.0062.
Values may be sent and summed in bfloat16 or wider, within the bound.
No kernel may reach another device: no remote copies, remote signals or barrier semaphores. Data moves between devices by JAX's collectives and lax.ppermute only.
A program may use at most 128 MiB of HBM per device.

v0:
```python
import jax
import jax.numpy as jnp
from jax import lax
from jax.sharding import PartitionSpec as P

SIDE = 192
BLOCK = 2
STEPS = 2
TGT_DEV = 1


COUL = 160.0


def broadcast(block, axis, holder):
    block = jnp.where(lax.axis_index(axis) == holder, block, jnp.zeros_like(block))
    return lax.psum(block, axis)


def cas_matrix(count):
    indices = jnp.arange(count, dtype=jnp.int32)
    products = indices[:, None] * indices[None, :] % count
    phases = products.astype(jnp.float32) * (2.0 * jnp.pi / count)
    return (jnp.cos(phases) + jnp.sin(phases)).astype(jnp.bfloat16)


def kernel_columns(count, first_row, rows_here):
    indices = jnp.arange(count, dtype=jnp.int32)
    wave_num = jnp.where(indices < count // 2, indices, indices - count).astype(jnp.float32)
    local_rows = jnp.arange(rows_here, dtype=jnp.int32) + first_row
    wave_mid = jnp.where(local_rows < count // 2, local_rows, local_rows - count).astype(
        jnp.float32
    )
    squared = wave_num * wave_num
    norm_sq = squared[:, None, None] + (wave_mid * wave_mid)[None, :, None] + squared[None, None, :]
    bounded = jnp.maximum(norm_sq, 1.0)
    return jnp.where(norm_sq > 0.5, COUL / bounded, 0.0) / float(count) ** 3


def convolve(density, cas_table):
    along_z = jnp.einsum(
        "pxyz,kz->pxyk", density, cas_table, preferred_element_type=jnp.float32
    ).astype(jnp.bfloat16)
    along_y = jnp.einsum(
        "pxyz,ky->pxkz", along_z, cas_table, preferred_element_type=jnp.float32
    ).astype(jnp.bfloat16)
    columns = lax.all_to_all(along_y, "grid", split_axis=2, concat_axis=1, tiled=True)
    rows_here = columns.shape[2]
    first_row = lax.axis_index("grid") * rows_here
    kernel = kernel_columns(SIDE, first_row, rows_here)
    summed = jnp.einsum("pxyz,kx->pkyz", columns, cas_table, preferred_element_type=jnp.float32)
    spectrum = (kernel[None] * summed).astype(jnp.bfloat16)
    back_x = jnp.einsum(
        "pkyz,xk->pxyz", spectrum, cas_table, preferred_element_type=jnp.float32
    ).astype(jnp.bfloat16)
    back_planes = lax.all_to_all(back_x, "grid", split_axis=1, concat_axis=2, tiled=True)
    back_y = jnp.einsum(
        "pxkz,yk->pxyz", back_planes, cas_table, preferred_element_type=jnp.float32
    ).astype(jnp.bfloat16)
    return jnp.einsum("pxyk,zk->pxyz", back_y, cas_table, preferred_element_type=jnp.float32)


def fetch_sources(orbitals, root_band):
    return broadcast(orbitals, "band", root_band)


def local(orbitals):
    planes = orbitals.shape[1]
    cas_table = cas_matrix(SIDE)
    targets = orbitals[:TGT_DEV].reshape(TGT_DEV, planes, SIDE, SIDE).astype(jnp.float32)
    result = jnp.zeros((TGT_DEV, planes, SIDE, SIDE), jnp.float32)
    groups = lax.axis_size("band")
    for step_no in range(STEPS):
        sources = (
            fetch_sources(orbitals, step_no * groups // STEPS)
            .reshape(BLOCK, planes, SIDE, SIDE)
            .astype(jnp.float32)
        )
        density = (targets[:, None] * sources[None]).astype(jnp.bfloat16)
        density = density.reshape(TGT_DEV * BLOCK, planes, SIDE, SIDE)
        potential = convolve(density, cas_table).reshape(TGT_DEV, BLOCK, planes, SIDE, SIDE)
        result = result - jnp.sum(potential * sources[None], axis=1)
    return result.reshape(TGT_DEV, planes, SIDE * SIDE)


def solution(mesh):
    return jax.shard_map(
        local,
        mesh=mesh,
        in_specs=(P("band", "grid", None),),
        out_specs=P("band", "grid", None),
        check_vma=False,
    )
```

profile of v0, /device:TPU:32, one launch (start us, length us, event | category | flops | bytes accessed | tf_op | source)
XLA Modules:
  0.0 643.6 jit_solution(7901450250336772781)
XLA Ops:
  10.8 8.4 %convert_element_type.172 = bf16[2,24,192,192]{3,2,1,0:T(8,128)(2,1)} reshape(bf16[2,24,36864]{2,1,0:T(8,128)(2,1)} %get-tuple-element.7) | data formatting | bytes 7077888 | tf_op jit(solution)/shard_map/convert_element_type | solution.py:77
  19.2 6.4 convert_element_type.184
  31.1 326.3 %all-reduce.3.cloned.1.call-done = (bf16[2,24,192,192]{3,2,1,0:T(8,128)(2,1)}, bf16[2,24,192,192]{3,2,1,0:T(8,128)(2,1)}) async-done(((bf16[2,24,192,192]{3,2,1,0:T(8,128)(2,1)}, bf16[2,24,192,192]{3,2,1,0:T(8,128)(2,1)}), (bf16[2,24,192,192]{3,2,1,0:T(8,128)(2,1)}, bf16[2,24,192,192]{3,2,1,0:T(8,128)(2,1)})) %all-reduce.3.cloned.1.call-update) | async-done | bytes 7077904 | tf_op jit(solution)/shard_map/psum | solution.py:17
  357.5 9.5 %convert_bitcast_fusion.1 = bf16[2,24,192,192]{3,2,1,0:T(8,128)(2,1)} fusion(bf16[2,24,192,192]{3,2,1,0:T(8,128)(2,1)} %get-tuple-element.5, f32[24,192,192]{2,1,0:T(8,128)} %reshape.132), kind=kOutput, calls=%fused_computation.31 | convolution fusion | flops 1368612864 | bytes 10616832 | tf_op jit(solution)/shard_map/pxyz,ky->pxkz/dot_general | solution.py:44
  367.0 7.1 %copy.19 = bf16[2,24,192,192]{3,1,0,2:T(8,128)(2,1)} copy(bf16[2,24,192,192]{3,2,1,0:T(8,128)(2,1)} %convert_bitcast_fusion.1) | data formatting | bytes 7077888 | tf_op jit(solution)/shard_map/convert_element_type | solution.py:46
  374.1 8.2 %all-to-all-start.2 = ((bf16[2,24,192,192]{3,1,0,2:T(8,128)(2,1)}), bf16[2,24,192,192]{3,1,0,2:T(8,128)(2,1)}, u32[]{:S(2)}, u32[]{:S(2)}) async-start(bf16[2,24,192,192]{3,1,0,2:T(8,128)(2,1)} %copy.19), calls=%async_computation.2 | async-start | bytes 9437184 | tf_op jit(solution)/shard_map/all_to_all | solution.py:47
  382.3 9.5 %convert_bitcast_fusion.3 = bf16[2,24,192,192]{3,2,1,0:T(8,128)(2,1)} fusion(bf16[2,24,192,192]{3,2,1,0:T(8,128)(2,1)} %get-tuple-element.6, f32[24,192,192]{2,1,0:T(8,128)} %reshape.132), kind=kOutput, calls=%fused_computation.37 | convolution fusion | flops 1368612864 | bytes 10616832 | tf_op jit(solution)/shard_map/pxyz,ky->pxkz/dot_general | solution.py:44
  391.8 7.2 %copy.12 = bf16[2,24,192,192]{3,1,0,2:T(8,128)(2,1)} copy(bf16[2,24,192,192]{3,2,1,0:T(8,128)(2,1)} %convert_bitcast_fusion.3) | data formatting | bytes 7077888 | tf_op jit(solution)/shard_map/convert_element_type | solution.py:46
  399.0 35.1 %all-to-all-done.2 = bf16[2,24,192,192]{3,1,0,2:T(8,128)(2,1)} async-done(((bf16[2,24,192,192]{3,1,0,2:T(8,128)(2,1)}), bf16[2,24,192,192]{3,1,0,2:T(8,128)(2,1)}, u32[]{:S(2)}, u32[]{:S(2)}) %all-to-all-start.2) | async-done | bytes 3538976 | tf_op jit(solution)/shard_map/all_to_all | solution.py:47
  434.1 6.2 all-to-all-start
  443.3 6.2 copy.21
  449.4 9.7 %convert_bitcast_fusion = bf16[2,192,24,192]{3,1,2,0:T(8,128)(2,1)} fusion(f32[192,24,192]{2,0,1:T(8,128)} %fusion.6, bf16[2,192,24,192]{3,2,1,0:T(8,128)(2,1)} %bitcast.63), kind=kOutput, calls=%fused_computation.30 | convolution fusion | flops 1365073920 | bytes 10616832 | tf_op jit(solution)/shard_map/pkyz,xk->pxyz/dot_general | solution.py:53
  459.1 7.2 %copy.23 = bf16[2,192,24,192]{3,2,0,1:T(8,128)(2,1)} copy(bf16[2,192,24,192]{3,1,2,0:T(8,128)(2,1)} %convert_bitcast_fusion) | data formatting | bytes 7077888 | tf_op jit(solution)/shard_map/convert_element_type | solution.py:55
  466.4 26.3 %all-to-all-done = bf16[2,24,192,192]{3,1,0,2:T(8,128)(2,1)} async-done(((bf16[2,24,192,192]{3,1,0,2:T(8,128)(2,1)}), bf16[2,24,192,192]{3,1,0,2:T(8,128)(2,1)}, u32[]{:S(2)}, u32[]{:S(2)}) %all-to-all-start) | async-done | bytes 3538976 | tf_op jit(solution)/shard_map/all_to_all | solution.py:47
  498.5 6.2 copy.14
  504.7 9.7 %convert_bitcast_fusion.2 = bf16[2,192,24,192]{3,1,2,0:T(8,128)(2,1)} fusion(f32[192,24,192]{2,0,1:T(8,128)} %fusion.6, bf16[2,192,24,192]{3,2,1,0:T(8,128)(2,1)} %bitcast.62), kind=kOutput, calls=%fused_computation.36 | convolution fusion | flops 1365073920 | bytes 10616832 | tf_op jit(solution)/shard_map/pkyz,xk->pxyz/dot_general | solution.py:53
  514.4 7.1 %copy.16 = bf16[2,192,24,192]{3,2,0,1:T(8,128)(2,1)} copy(bf16[2,192,24,192]{3,1,2,0:T(8,128)(2,1)} %convert_bitcast_fusion.2) | data formatting | bytes 7077888 | tf_op jit(solution)/shard_map/convert_element_type | solution.py:55
  521.5 29.3 %all-to-all-done.3 = bf16[2,192,24,192]{3,2,0,1:T(8,128)(2,1)} async-done(((bf16[2,192,24,192]{3,2,0,1:T(8,128)(2,1)}), bf16[2,192,24,192]{3,2,0,1:T(8,128)(2,1)}, u32[]{:S(2)}, u32[]{:S(2)}) %all-to-all-start.3) | async-done | bytes 3538976 | tf_op jit(solution)/shard_map/all_to_all | solution.py:56
  550.8 5.9 all-to-all-start.1
  561.9 9.7 %fusion.3 = f32[24,192,192]{2,1,0:T(8,128)} fusion(bf16[2,24,192,192]{3,2,1,0:T(8,128)(2,1)} %get-tuple-element.5, bf16[2,24,192,192]{3,2,1,0:T(8,128)(2,1)} %bitcast.64), kind=kOutput, calls=%fused_computation.7 | convolution fusion | flops 1365958656 | bytes 10616832 | tf_op jit(solution)/shard_map/pxyk,zk->pxyz/dot_general | solution.py:60
  571.6 37.5 %all-to-all-done.1 = bf16[2,192,24,192]{3,2,0,1:T(8,128)(2,1)} async-done(((bf16[2,192,24,192]{3,2,0,1:T(8,128)(2,1)}), bf16[2,192,24,192]{3,2,0,1:T(8,128)(2,1)}, u32[]{:S(2)}, u32[]{:S(2)}) %all-to-all-start.1) | async-done | bytes 3538976 | tf_op jit(solution)/shard_map/all_to_all | solution.py:56
  614.2 9.6 %fusion.1 = f32[24,192,192]{2,1,0:T(8,128)} fusion(bf16[2,24,192,192]{3,2,1,0:T(8,128)(2,1)} %get-tuple-element.6, bf16[2,24,192,192]{3,2,1,0:T(8,128)(2,1)} %bitcast.65), kind=kOutput, calls=%fused_computation.5 | convolution fusion | flops 1365958656 | bytes 10616832 | tf_op jit(solution)/shard_map/pxyk,zk->pxyz/dot_general | solution.py:60
  623.8 6.8 %subtract_subtract_fusion = f32[24,192,192]{2,1,0:T(8,128)} fusion(f32[24,192,192]{2,1,0:T(8,128)} %fusion.3, f32[24,192,192]{2,1,0:T(8,128)} %fusion.1), kind=kLoop, calls=%fused_computation.34 | loop fusion | flops 1769472 | bytes 10616832 | tf_op jit(solution)/shard_map/sub | solution.py:82
  630.6 5.9 sub.42
  (12 shorter events, 28.8 us)
Async XLA Ops:
  6.5 351.0 %all-reduce.3.cloned.1.call-start = ((), (), s32[]{:S(2)}) async-start(), calls=%async_computation.4 | async-start | bytes 18874368 | tf_op jit(solution)/shard_map/psum | solution.py:17
  374.1 60.0 %all-to-all-start.2 = ((bf16[2,24,192,192]{3,1,0,2:T(8,128)(2,1)}), bf16[2,24,192,192]{3,1,0,2:T(8,128)(2,1)}, u32[]{:S(2)}, u32[]{:S(2)}) async-start(bf16[2,24,192,192]{3,1,0,2:T(8,128)(2,1)} %copy.19), calls=%async_computation.2 | async-start | bytes 9437184 | tf_op jit(solution)/shard_map/all_to_all | solution.py:47
  434.1 58.5 %all-to-all-start = ((bf16[2,24,192,192]{3,1,0,2:T(8,128)(2,1)}), bf16[2,24,192,192]{3,1,0,2:T(8,128)(2,1)}, u32[]{:S(2)}, u32[]{:S(2)}) async-start(bf16[2,24,192,192]{3,1,0,2:T(8,128)(2,1)} %copy.12), calls=%async_computation | async-start | bytes 9437184 | tf_op jit(solution)/shard_map/all_to_all | solution.py:47
  492.6 58.2 %all-to-all-start.3 = ((bf16[2,192,24,192]{3,2,0,1:T(8,128)(2,1)}), bf16[2,192,24,192]{3,2,0,1:T(8,128)(2,1)}, u32[]{:S(2)}, u32[]{:S(2)}) async-start(bf16[2,192,24,192]{3,2,0,1:T(8,128)(2,1)} %copy.23), calls=%async_computation.3 | async-start | bytes 9437184 | tf_op jit(solution)/shard_map/all_to_all | solution.py:56
  550.8 58.2 %all-to-all-start.1 = ((bf16[2,192,24,192]{3,2,0,1:T(8,128)(2,1)}), bf16[2,192,24,192]{3,2,0,1:T(8,128)(2,1)}, u32[]{:S(2)}, u32[]{:S(2)}) async-start(bf16[2,192,24,192]{3,2,0,1:T(8,128)(2,1)} %copy.16), calls=%async_computation.1 | async-start | bytes 9437184 | tf_op jit(solution)/shard_map/all_to_all | solution.py:56
Sparse Core Ops, SparseCore 0:
  25.8 331.6 all-reduce.2
where the time goes:
time: 656 us; the launch traced here: 644 us
  waiting for transfers between devices  455 us (69%)
  local copies, waits for them, and re-layouts  75.7 us (12%)
  matrix products  57.7 us (9%)
  starting transfers between devices  26.2 us (4%)
  other arithmetic  15.7 us (2%)
  between operations  13.7 us (2%)
    psum x1, waiting for transfers between devices, broadcast(): return lax.psum(block, axis)  326 us
    all_to_all x2, waiting for transfers between devices, convolve(): lax.all_to_all(back_x, 'grid', split_axis=1, concat_axis=2, tiled=True)  66.8 us
    all_to_all x2, waiting for transfers between devices, convolve(): lax.all_to_all(along_y, 'grid', split_axis=2, concat_axis=1, tiled=True)  61.4 us
    dot_general x2, matrix products, convolve(): jnp.einsum('pkyz,xk->pxyz', spectrum, cas_table, preferred_element_type=j...  19.4 us
    dot_general x2, matrix products, convolve(): jnp.einsum('pxyk,zk->pxyz', back_y, cas_table, preferred_element_type=jnp...  19.3 us
    dot_general x2, matrix products, convolve(): jnp.einsum('pxyz,ky->pxkz', along_z, cas_table, preferred_element_type=jn...  19 us
    convert_element_type x2, local copies, waits for them, and re-layouts, local(): sources = fetch_sources(orbitals, step_no * groups // STEPS).reshape(BLOC...  14.8 us
    all_to_all x2, starting transfers between devices, convolve(): lax.all_to_all(along_y, 'grid', split_axis=2, concat_axis=1, tiled=True)  14.4 us
  transfers between devices with their start and end apart: 5, of which 5 were waited for; matrix products, arithmetic and copies ran while one was open for 13% of the time, Pallas kernels for 0%

commit v1 on v0

v1 whole, which is shorter than its diff:
```python
import jax
import jax.numpy as jnp
from jax import lax
from jax.experimental import pallas as pl
from jax.experimental.pallas import tpu as pltpu
from jax.sharding import PartitionSpec as P

SIDE = 192
PARTS = 8
ROWS = SIDE // PARTS
QUADS = ROWS // 4
COUL = 160.0
F32 = jnp.float32
BF16 = jnp.bfloat16


def cas_of(left, right):
    products = left[:, None] * right[None, :] % SIDE
    phases = products.astype(F32) * (2.0 * jnp.pi / SIDE)
    return (jnp.cos(phases) + jnp.sin(phases)).astype(BF16)


def wave(index):
    return jnp.where(index < SIDE // 2, index, index - SIDE).astype(F32)


def tables(me):
    natural = jnp.arange(SIDE, dtype=jnp.int32)
    partner = me ^ jnp.arange(PARTS, dtype=jnp.int32)
    by_partner = (partner[:, None] * ROWS + jnp.arange(ROWS, dtype=jnp.int32)[None]).reshape(-1)
    stacked = by_partner.reshape(SIDE // 2, 2).T.reshape(-1)
    return cas_of(by_partner, natural), cas_of(natural, by_partner), cas_of(natural, stacked), cas_of(stacked, natural)


def z_tables():
    natural = jnp.arange(SIDE, dtype=jnp.int32)
    cas = cas_of(natural, natural)
    gap = jnp.zeros((SIDE, 64), BF16)
    first = jnp.concatenate([cas, gap], axis=1)
    second = jnp.concatenate([cas[:, :128], gap, cas[:, 128:]], axis=1)
    return first, second, first.T, second.T


def coulomb(me):
    shape = (ROWS // 2, SIDE, 384)
    pair = lax.broadcasted_iota(jnp.int32, shape, 0)
    row = lax.broadcasted_iota(jnp.int32, shape, 1)
    col = lax.broadcasted_iota(jnp.int32, shape, 2)
    late = jnp.where(col < 256, col >= 128, col >= 320)
    kz = jnp.where(col < 256, col % 128, 128 + col % 64)
    ky = me * ROWS + pair + jnp.where(late, ROWS // 2, 0)
    mx, my, mz = wave(row), wave(ky), wave(kz)
    norm_sq = mx * mx + my * my + mz * mz
    bounded = jnp.maximum(norm_sq, 1.0)
    return jnp.where(norm_sq > 0.5, COUL / bounded, 0.0) / float(SIDE) ** 3


def dot(left, right):
    return jnp.dot(left, right, preferred_element_type=F32)


def forward_body(target, source, z_first, z_second, y_table, *outs):
    lanes = []
    for pair in range(2):
        halves = []
        for plane, table in ((2 * pair, z_first), (2 * pair + 1, z_second)):
            density = (target[plane].astype(F32) * source[0, plane].astype(F32)).astype(BF16)
            halves.append(dot(density, table[...]))
        low, high = halves
        packed = jnp.concatenate([low[:, :128], high[:, :128], low[:, 128:] + high[:, 128:]], axis=1)
        lanes.append(dot(y_table[...], packed.astype(BF16)))
    for part, out in enumerate(outs):
        rows = slice(part * ROWS, (part + 1) * ROWS)
        out[0, 0] = jnp.concatenate([lanes[0][rows], lanes[1][rows]], axis=0).astype(BF16)


def whole(shape):
    return pl.BlockSpec(shape, lambda *_: (0,) * len(shape))


def forward(target, sources, z_first, z_second, y_table):
    pairs = sources.shape[0]
    piece = jax.ShapeDtypeStruct((pairs, QUADS, 2 * ROWS, 384), BF16)
    return pl.pallas_call(
        forward_body,
        grid=(pairs, QUADS),
        in_specs=[
            pl.BlockSpec((4, SIDE, SIDE), lambda p, q: (q, 0, 0)),
            pl.BlockSpec((1, 4, SIDE, SIDE), lambda p, q: (p, q, 0, 0)),
            whole((SIDE, 256)),
            whole((SIDE, 256)),
            whole((SIDE, SIDE)),
        ],
        out_specs=[pl.BlockSpec((1, 1, 2 * ROWS, 384), lambda p, q: (p, q, 0, 0))] * PARTS,
        out_shape=[piece] * PARTS,
        compiler_params=pltpu.CompilerParams(vmem_limit_bytes=32 * 2**20),
        cost_estimate=pl.CostEstimate(flops=pairs * 1400 * 10**6, bytes_accessed=pairs * 7 * 10**6, transcendentals=0),
        name="forward_zy",
    )(target, sources, z_first, z_second, y_table)


def middle_body(*refs):
    ins, (kernel, x_table, x_back), outs, (head0, head1, tail) = refs[:8], refs[8:11], refs[11:19], refs[19:]
    lots = (head0, head1, tail)
    block = QUADS * 2 * ROWS
    for part, ref in enumerate(ins):
        for tile, lot in enumerate(lots):
            lot[part * block : (part + 1) * block] = (
                ref[0, :, :, tile * 128 : (tile + 1) * 128].astype(F32).reshape(block, 128)
            )
    low = lax.broadcasted_iota(jnp.int32, (96, 128), 1) < 64

    def step(i, carry):
        here = pl.ds(i, 96, stride=ROWS)
        there = pl.ds(i + ROWS // 2, 96, stride=ROWS)
        tail_a, tail_b = tail[here, :], tail[there, :]
        tail_first = jnp.where(low, tail_a, pltpu.roll(tail_b, 64, 1))
        tail_second = jnp.where(low, pltpu.roll(tail_a, 64, 1), tail_b)
        columns = jnp.concatenate(
            [
                jnp.concatenate([head0[here, :], head0[there, :], tail_first], axis=1),
                jnp.concatenate([head1[here, :], head1[there, :], tail_second], axis=1),
            ],
            axis=0,
        ).astype(BF16)
        spectrum = (kernel[i] * dot(x_table[...], columns)).astype(BF16)
        back = dot(x_back[...], spectrum)
        head0[here, :] = back[:96, :128]
        head1[here, :] = back[96:, :128]
        head0[there, :] = back[:96, 128:256]
        head1[there, :] = back[96:, 128:256]
        first, second = back[:96, 256:], back[96:, 256:]
        tail[here, :] = jnp.where(low, first, pltpu.roll(second, 64, 1))
        tail[there, :] = jnp.where(low, pltpu.roll(first, 64, 1), second)
        return carry

    lax.fori_loop(0, ROWS // 2, step, 0)
    for part, ref in enumerate(outs):
        for tile, lot in enumerate(lots):
            ref[0, :, :, tile * 128 : (tile + 1) * 128] = (
                lot[part * block : (part + 1) * block].astype(BF16).reshape(QUADS, 2 * ROWS, 128)
            )


def middle(pieces, kernel, x_table, x_back):
    pairs = pieces[0].shape[0]
    spec = pl.BlockSpec((1, QUADS, 2 * ROWS, 384), lambda p: (p, 0, 0, 0))
    return pl.pallas_call(
        middle_body,
        grid=(pairs,),
        in_specs=[spec] * PARTS + [whole(kernel.shape), whole((SIDE, SIDE)), whole((SIDE, SIDE))],
        out_specs=[spec] * PARTS,
        out_shape=[jax.ShapeDtypeStruct(pieces[0].shape, BF16)] * PARTS,
        scratch_shapes=[pltpu.VMEM((SIDE // 2 * ROWS, 128), F32)] * 3,
        compiler_params=pltpu.CompilerParams(vmem_limit_bytes=40 * 2**20),
        cost_estimate=pl.CostEstimate(flops=pairs * 1400 * 10**6, bytes_accessed=pairs * 7 * 10**6, transcendentals=0),
        name="middle_x",
    )(*pieces, kernel, x_table, x_back)


def backward_body(*refs):
    ins, (sources, total, y_table, z_first, z_second), out = refs[:8], refs[8:13], refs[13]
    pairs = sources.shape[0]
    for pair in range(2):
        sums = [total[2 * pair], total[2 * pair + 1]]
        for which in range(pairs):
            rows = slice(pair * ROWS, (pair + 1) * ROWS)
            stack = jnp.concatenate([ref[which, 0].astype(F32)[rows] for ref in ins], axis=0).astype(BF16)
            planes = dot(y_table[...], stack).astype(BF16)
            first = dot(jnp.concatenate([planes[:, :128], planes[:, 256:]], axis=1), z_first[...])
            second = dot(planes[:, 128:], z_second[...])
            sums[0] = sums[0] - first * sources[which, 2 * pair].astype(F32)
            sums[1] = sums[1] - second * sources[which, 2 * pair + 1].astype(F32)
        out[2 * pair] = sums[0]
        out[2 * pair + 1] = sums[1]


def backward(pieces, sources, total, y_table, z_first, z_second):
    pairs = sources.shape[0]
    piece = pl.BlockSpec((pairs, 1, 2 * ROWS, 384), lambda q: (0, q, 0, 0))
    wide = pl.BlockSpec((4, SIDE, SIDE), lambda q: (q, 0, 0))
    return pl.pallas_call(
        backward_body,
        grid=(QUADS,),
        in_specs=[piece] * PARTS
        + [
            pl.BlockSpec((pairs, 4, SIDE, SIDE), lambda q: (0, q, 0, 0)),
            wide,
            whole((SIDE, SIDE)),
            whole((256, SIDE)),
            whole((256, SIDE)),
        ],
        out_specs=wide,
        out_shape=jax.ShapeDtypeStruct((ROWS, SIDE, SIDE), F32),
        compiler_params=pltpu.CompilerParams(vmem_limit_bytes=40 * 2**20),
        cost_estimate=pl.CostEstimate(flops=pairs * 1400 * 10**6, bytes_accessed=pairs * 7 * 10**6, transcendentals=0),
        name="backward_yz",
    )(*pieces, sources, total, y_table, z_first, z_second)


def exchange(pieces):
    return [pieces[0]] + [
        lax.ppermute(pieces[d], "grid", [(i, i ^ d) for i in range(PARTS)]) for d in range(1, PARTS)
    ]


def band_of(z_hi, x, core):
    return z_hi * 8 + x * 2 + core


def spread(orbitals):
    band = lax.axis_index("band")
    z_hi, x = band // 8, (band // 2) % 4
    core = band % 2
    cut = orbitals.shape[2] // 4
    chunks = orbitals.reshape(2, ROWS, 4, cut)
    mine = jnp.where(x == 0, chunks[:, :, 0], jnp.zeros((), BF16))
    for step in range(1, 4):
        pairs = [(band_of(z, 0, 0), band_of(z, step, 0)) for z in (0, 2)]
        mine = mine + lax.ppermute(chunks[:, :, step], "band", pairs)
    swap = [(band_of(z, i, 0), band_of(z, i, 1)) for z in (0, 2) for i in range(4)]
    other = lax.ppermute(mine[..., cut // 2 :], "band", swap)
    mine = jnp.where(core == 0, mine[..., : cut // 2], other)
    got = []
    for moves in (((0, 1), (2, 3)), ((0, 3), (2, 1)), ((0, 2), (2, 0))):
        pairs = [(band_of(a, i, c), band_of(b, i, c)) for a, b in moves for i in range(4) for c in range(2)]
        got.append(lax.ppermute(mine, "band", pairs))
    near, far, cross = got
    from_first = jnp.where(z_hi == 0, mine, jnp.where(z_hi == 1, near, jnp.where(z_hi == 2, cross, far)))
    from_second = jnp.where(z_hi == 2, mine, jnp.where(z_hi == 3, near, jnp.where(z_hi == 0, cross, far)))
    both = jnp.stack([from_first, from_second], axis=1)
    groups = [[8 * k + i for i in range(8)] for k in range(4)]
    gathered = [
        lax.all_gather(both[p], "band", axis=0, axis_index_groups=groups)
        for p in range(2)
    ]
    return [
        jnp.moveaxis(g.reshape(8, 2, ROWS, ROWS, SIDE), 0, 2).reshape(2, ROWS, SIDE, SIDE) for g in gathered
    ]


def local(orbitals):
    me = lax.axis_index("grid")
    y_table, y_back, x_table, x_back = tables(me)
    z_first, z_second, z_first_back, z_second_back = z_tables()
    kernel = coulomb(me)
    target = orbitals[0].reshape(ROWS, SIDE, SIDE)
    total = jnp.zeros((ROWS, SIDE, SIDE), F32)
    batches = spread(orbitals)
    backs = []
    for sources in batches:
        pieces = exchange(forward(target, sources, z_first, z_second, y_table))
        backs.append(exchange(middle(pieces, kernel, x_table, x_back)))
    for pieces, sources in zip(backs, batches):
        total = backward(pieces, sources, total, y_back, z_first_back, z_second_back)
    return total.reshape(1, ROWS, SIDE * SIDE)


def solution(mesh):
    return jax.shard_map(
        local,
        mesh=mesh,
        in_specs=(P("band", "grid", None),),
        out_specs=P("band", "grid", None),
        check_vma=False,
    )
```

time: 656 us -> 388 us (0.59); the launches traced: 644 us -> 385 us
  waiting for transfers between devices: 455 us -> 144 us
  Pallas kernels: 0 us -> 64.2 us
  matrix products: 57.7 us -> 0 us
  starting transfers between devices: 26.2 us -> 64.4 us
    psum x1 -> x0, waiting for transfers between devices: 326 us -> none  [broadcast(): return lax.psum(block, axis)]
    all_to_all x4 -> x0, waiting for transfers between devices: 128 us -> none  [the longest x2 66.8 us: convolve(): lax.all_to_all(back_x, 'grid', split_axis=1, concat_axis=2, tiled=True)]
    ppermute x0 -> x35, waiting for transfers between devices: none -> 112 us  [the longest x28 76.8 us: exchange(): lax.ppermute(pieces[d], 'grid', [(i, i ^ d) for i in range(PARTS)])]
    ppermute x0 -> x35, starting transfers between devices: none -> 64.4 us  [the longest x28 43 us: exchange(): lax.ppermute(pieces[d], 'grid', [(i, i ^ d) for i in range(PARTS)])]
    pallas_call x0 -> x6, Pallas kernels: none -> 64.2 us  [the longest x2 30.6 us: middle(): pl.pallas_call(middle_body, grid=(pairs,), in_specs=[spec] * PARTS + [who...]
    dot_general x6 -> x0, matrix products: 57.7 us -> none  [the longest x2 19.4 us: convolve(): jnp.einsum('pkyz,xk->pxyz', spectrum, cas_table, preferred_element_type=j...]
    convert_element_type x7 -> x4, local copies, waits for them, and re-layouts: 47.3 us -> 4.35 us  [cas_of(): return (jnp.cos(phases) + jnp.sin(phases)).astype(BF16)]
    reshape x0 -> x6, local copies, waits for them, and re-layouts: none -> 32.8 us  [the longest x4 21.8 us: spread(): g.reshape(8, 2, ROWS, ROWS, SIDE)]
  transfers between devices with their start and end apart: 5 -> 37, of which waited for: 5 -> 12; matrix products, arithmetic and copies ran while one was open for 13% -> 13% of each run, Pallas kernels for 0% -> 15%
where the time goes in v1:
time: 388 us; the launch traced here: 385 us
  waiting for transfers between devices  144 us (37%)
  local copies, waits for them, and re-layouts  75.7 us (20%)
  starting transfers between devices  64.4 us (17%)
  Pallas kernels  64.2 us (17%)
  other arithmetic  22.1 us (6%)
  between operations  14 us (4%)
    ppermute x28, waiting for transfers between devices, exchange(): lax.ppermute(pieces[d], 'grid', [(i, i ^ d) for i in range(PARTS)])  76.8 us
    ppermute x28, starting transfers between devices, exchange(): lax.ppermute(pieces[d], 'grid', [(i, i ^ d) for i in range(PARTS)])  43 us
    all_gather x2, waiting for transfers between devices, spread(): lax.all_gather(both[p], 'band', axis=0, axis_index_groups=groups)  32.1 us
    pallas_call x2, Pallas kernels, middle(): pl.pallas_call(middle_body, grid=(pairs,), in_specs=[spec] * PARTS + [who...  30.6 us
    unnamed x108, local copies, waits for them, and re-layouts  28.3 us
    reshape x4, local copies, waits for them, and re-layouts, spread(): g.reshape(8, 2, ROWS, ROWS, SIDE)  21.8 us
    ppermute x3, waiting for transfers between devices, spread(): got.append(lax.ppermute(mine, 'band', pairs))  18.1 us
    pallas_call x2, Pallas kernels, forward(): pl.pallas_call(forward_body, grid=(pairs, QUADS), in_specs=[pl.BlockSpec(...  17.9 us
  transfers between devices with their start and end apart: 37, of which 12 were waited for; matrix products, arithmetic and copies ran while one was open for 13% of the time, Pallas kernels for 15%

profile of v1, /device:TPU:32, one launch (start us, length us, event | category | flops | bytes accessed | tf_op | source)
XLA Modules:
  0.0 384.9 jit_solution(10577559188703079739)
XLA Ops:
  6.5 5.1 %reshape.59 = bf16[2,24,4,9216]{3,2,1,0:T(4,128)(2,1)S(1)} reshape(bf16[2,24,36864]{2,1,0:T(8,128)(2,1)} %param.1) | data formatting | bytes 7077888 | tf_op jit(solution)/shard_map/reshape | solution.py:216
  11.7 6.3 %broadcast_select_fusion = (bf16[2,24,1,9216]{3,2,1,0:T(2,128)(2,1)S(1)}, bf16[2,24,1,9216]{3,2,1,0:T(2,128)(2,1)S(1)}, bf16[2,24,1,9216]{3,2,1,0:T(2,128)(2,1)S(1)}, bf16[2,24,1,9216]{3,2,1,0:T(2,128)(2,1)S(1)}) fusion(pred[]{:T(512)S(6)} %eq.34, bf16[2,24,4,9216]{3,2,1,0:T(4,128)(2,1)S(1)} %reshape.59), kind=kLoop, calls=%fused_computation.9 | loop fusion | flops 442368 | bytes 7077889 | tf_op jit(solution)/shard_map/jit(_where)/select_n | solution.py:217
  26.0 6.3 %collective-permute-done = bf16[2,24,9216]{2,1,0:T(8,128)(2,1)S(1)} collective-permute-done((bf16[2,24,9216]{2,1,0:T(8,128)(2,1)S(1)}, bf16[2,24,9216]{2,1,0:T(8,128)(2,1)S(1)}, u32[]{:S(2)}, u32[]{:S(2)}) %collective-permute-start) | collective-permute-done | bytes 884768 | tf_op jit(solution)/shard_map/ppermute | solution.py:220
  32.3 9.5 %collective-permute-done.1 = bf16[2,24,9216]{2,1,0:T(8,128)(2,1)S(1)} collective-permute-done((bf16[2,24,9216]{2,1,0:T(8,128)(2,1)S(1)}, bf16[2,24,9216]{2,1,0:T(8,128)(2,1)S(1)}, u32[]{:S(2)}, u32[]{:S(2)}) %collective-permute-start.1) | collective-permute-done | bytes 884768 | tf_op jit(solution)/shard_map/ppermute | solution.py:220
  50.9 8.2 %collective-permute-start.5 = (bf16[2,24,4608]{2,1,0:T(8,128)(2,1)}, bf16[2,24,4608]{2,1,0:T(8,128)(2,1)}, u32[]{:S(2)}, u32[]{:S(2)}) collective-permute-start(bf16[2,24,4608]{2,1,0:T(8,128)(2,1)} %slice_select_fusion), channel_id=1, source_target_pairs={{0,128},{8,136},{16,144},{24,152},{32,160},{40,168},{48,176},{56,1... | collective-permute-start | bytes 1327112 | tf_op jit(solution)/shard_map/ppermute | solution.py:227
  61.1 18.1 %collective-permute-done.4 = bf16[2,24,4608]{2,1,0:T(8,128)(2,1)} collective-permute-done((bf16[2,24,4608]{2,1,0:T(8,128)(2,1)}, bf16[2,24,4608]{2,1,0:T(8,128)(2,1)}, u32[]{:S(2)}, u32[]{:S(2)}) %collective-permute-start.4) | collective-permute-done | bytes 442400 | tf_op jit(solution)/shard_map/ppermute | solution.py:227
  91.9 4.0 %reshape_squeeze.3.target = bf16[24,192,192]{2,1,0:T(8,128)(2,1)S(1)} reshape(bf16[1,24,36864]{2,1,0:T(8,128)(2,1)} %slice.33) | data formatting | bytes 3538944 | tf_op jit(solution)/shard_map/reshape;squeeze | solution.py:247
  98.2 27.1 %all-gather.5.cloned.1.call-done = bf16[8,2,24,4608]{3,2,0,1:T(8,128)(2,1)} async-done(((bf16[1,2,24,4608]{3,2,0,1:T(8,128)(2,1)}), bf16[8,2,24,4608]{3,2,0,1:T(8,128)(2,1)}) %all-gather.5.cloned.1.call-update) | async-done | bytes 3538960 | tf_op jit(solution)/shard_map/all_gather | solution.py:234
  125.3 7.9 %reshape.62 = bf16[8,2,24,24,192]{4,3,2,0,1:T(8,128)(2,1)} reshape(bf16[8,2,24,4608]{3,2,0,1:T(8,128)(2,1)} %all-gather.5.cloned.1.call-done) | data formatting | bytes 7077888 | tf_op jit(solution)/shard_map/reshape | solution.py:238
  136.2 9.0 %forward_zy.3 = (bf16[2,6,48,384]{3,2,1,0:T(8,128)(2,1)S(1)}, bf16[2,6,48,384]{3,2,1,0:T(8,128)(2,1)}, bf16[2,6,48,384]{3,2,1,0:T(8,128)(2,1)}, bf16[2,6,48,384]...) custom-call(bf16[24,192,192]{2,1,0:T(8,128)(2,1)S(1)} %reshape_squee, ...), custom_call_target="tpu_custom_call" | custom-call | flops 2800000000 | bytes 14000000 | tf_op jit(solution)/shard_map/forward_zy/pallas_call | solution.py:84
  154.0 5.0 %all-gather.3.cloned.1.call-done = bf16[8,2,24,4608]{3,2,0,1:T(8,128)(2,1)} async-done(((bf16[1,2,24,4608]{3,2,0,1:T(8,128)(2,1)}), bf16[8,2,24,4608]{3,2,0,1:T(8,128)(2,1)}) %all-gather.3.cloned.1.call-update) | async-done | bytes 3538960 | tf_op jit(solution)/shard_map/all_gather | solution.py:234
  159.0 7.9 %reshape.60 = bf16[8,2,24,24,192]{4,3,2,0,1:T(8,128)(2,1)} reshape(bf16[8,2,24,4608]{3,2,0,1:T(8,128)(2,1)} %all-gather.3.cloned.1.call-done) | data formatting | bytes 7077888 | tf_op jit(solution)/shard_map/reshape | solution.py:238
  170.0 8.9 %forward_zy.2 = (bf16[2,6,48,384]{3,2,1,0:T(8,128)(2,1)S(1)}, bf16[2,6,48,384]{3,2,1,0:T(8,128)(2,1)S(1)}, bf16[2,6,48,384]{3,2,1,0:T(8,128)(2,1)S(1)}, bf16[2,6...) custom-call(bf16[24,192,192]{2,1,0:T(8,128)(2,1)S(1)} %reshape_squee, ...), custom_call_target="tpu_custom_call" | custom-call | flops 2800000000 | bytes 14000000 | tf_op jit(solution)/shard_map/forward_zy/pallas_call | solution.py:84
  195.6 31.8 %collective-permute-done.26.refs_6_ = bf16[2,6,48,384]{3,2,1,0:T(8,128)(2,1)} collective-permute-done((bf16[2,6,48,384]{3,2,1,0:T(8,128)(2,1)}, bf16[2,6,48,384]{3,2,1,0:T(8,128)(2,1)}, u32[]{:S(2)}, u32[]{:S(2)}) %collective-permute-start.26) | collective-permute-done | bytes 442400 | tf_op jit(solution)/shard_map/ppermute | solution.py:203
  243.0 14.8 %middle_x.3 = (bf16[2,6,48,384]{3,2,1,0:T(8,128)(2,1)S(1)}, bf16[2,6,48,384]{3,2,1,0:T(8,128)(2,1)S(1)}, bf16[2,6,48,384]{3,2,1,0:T(8,128)(2,1)S(1)}, bf16[2,6,4...) custom-call(bf16[2,6,48,384]{3,2,1,0:T(8,128)(2,1)S(1)} %copy-done.3, ...), custom_call_target="tpu_custom_call" | custom-call | flops 2800000000 | bytes 14000000 | tf_op jit(solution)/shard_map/middle_x/pallas_call | solution.py:148
  268.2 15.7 %middle_x.2 = (bf16[2,6,48,384]{3,2,1,0:T(8,128)(2,1)S(1)}, bf16[2,6,48,384]{3,2,1,0:T(8,128)(2,1)S(1)}, bf16[2,6,48,384]{3,2,1,0:T(8,128)(2,1)S(1)}, bf16[2,6,4...) custom-call(bf16[2,6,48,384]{3,2,1,0:T(8,128)(2,1)S(1)} %copy-done.3, ...), custom_call_target="tpu_custom_call" | custom-call | flops 2800000000 | bytes 14000000 | tf_op jit(solution)/shard_map/middle_x/pallas_call | solution.py:148
  286.2 6.0 %collective-permute-done.29.refs_2_ = bf16[2,6,48,384]{3,2,1,0:T(8,128)(2,1)S(1)} collective-permute-done((bf16[2,6,48,384]{3,2,1,0:T(8,128)(2,1)S(1)}, bf16[2,6,48,384]{3,2,1,0:T(8,128)(2,1)S(1)}, u32[]{:S(2)}, u32[]{:S(2)}) %collective-permute-start.29) | collective-permute-done | bytes 442400 | tf_op jit(solution)/shard_map/ppermute | solution.py:203
  295.8 12.7 %collective-permute-done.31.refs_4_ = bf16[2,6,48,384]{3,2,1,0:T(8,128)(2,1)S(1)} collective-permute-done((bf16[2,6,48,384]{3,2,1,0:T(8,128)(2,1)S(1)}, bf16[2,6,48,384]{3,2,1,0:T(8,128)(2,1)S(1)}, u32[]{:S(2)}, u32[]{:S(2)}) %collective-permute-start.31) | collective-permute-done | bytes 442400 | tf_op jit(solution)/shard_map/ppermute | solution.py:203
  312.0 5.9 %collective-permute-done.33.refs_6_ = bf16[2,6,48,384]{3,2,1,0:T(8,128)(2,1)S(1)} collective-permute-done((bf16[2,6,48,384]{3,2,1,0:T(8,128)(2,1)S(1)}, bf16[2,6,48,384]{3,2,1,0:T(8,128)(2,1)S(1)}, u32[]{:S(2)}, u32[]{:S(2)}) %collective-permute-start.33) | collective-permute-done | bytes 442400 | tf_op jit(solution)/shard_map/ppermute | solution.py:203
  324.8 14.1 %collective-permute-done.15.refs_2_ = bf16[2,6,48,384]{3,2,1,0:T(8,128)(2,1)S(1)} collective-permute-done((bf16[2,6,48,384]{3,2,1,0:T(8,128)(2,1)S(1)}, bf16[2,6,48,384]{3,2,1,0:T(8,128)(2,1)S(1)}, u32[]{:S(2)}, u32[]{:S(2)}) %collective-permute-start.15) | collective-permute-done | bytes 442400 | tf_op jit(solution)/shard_map/ppermute | solution.py:203
  345.8 7.8 %backward_yz.2.refs_9_ = f32[24,192,192]{2,1,0:T(8,128)S(1)} custom-call(bf16[2,6,48,384]{3,2,1,0:T(8,128)(2,1)S(1)} %copy-done.9, bf16[2,6,48,384]{3,2,1,0:T(8,128)(2,1)S(1)} %collective-permute-done.28.refs_1_, bf16[2,6,48,384]{3,2,1,0:T(8,128)(2,1)S(1)} %collective-permute-done.29.refs_2_, bf16[2,6,48,384]{3,2,1,0:T(8,128)(2,1)S(1)} %collective-permute-done.30.refs_3_, ...), custom_call_target="tpu_custom_call" | custom-call | flops 2800000000 | bytes 14000000 | tf_op jit(solution)/shard_map/backward_yz/pallas_call | solution.py:182
  355.8 6.1 %collective-permute-done.19.refs_6_ = bf16[2,6,48,384]{3,2,1,0:T(8,128)(2,1)} collective-permute-done((bf16[2,6,48,384]{3,2,1,0:T(8,128)(2,1)}, bf16[2,6,48,384]{3,2,1,0:T(8,128)(2,1)}, u32[]{:S(2)}, u32[]{:S(2)}) %collective-permute-start.19) | collective-permute-done | bytes 442400 | tf_op jit(solution)/shard_map/ppermute | solution.py:203
  362.0 7.9 %backward_yz.3 = f32[24,192,192]{2,1,0:T(8,128)S(1)} custom-call(bf16[2,6,48,384]{3,2,1,0:T(8,128)(2,1)S(1)} %get-tuple-element.45.refs_0_, bf16[2,6,48,384]{3,2,1,0:T(8,128)(2,1)S(1)} %copy-done.13, bf16[2,6,48,384]{3,2,1,0:T(8,128)(2,1)S(1)} %copy-done.15, bf16[2,6,48,384]{3,2,1,0:T(8,128)(2,1)} %collective-permute-done.16.refs_3_, ...), custom_call_target="tpu_custom_call" | custom-call | flops 2800000000 | bytes 14000000 | tf_op jit(solution)/shard_map/backward_yz/pallas_call | solution.py:182
  372.1 5.9 %reshape.64 = f32[1,24,36864]{2,1,0:T(8,128)} reshape(f32[24,192,192]{2,1,0:T(8,128)} %copy-done.3) | data formatting | bytes 7077888 | tf_op jit(solution)/shard_map/reshape | solution.py:256
  (218 shorter events, 118.6 us)
Async XLA Ops:
  6.5 118.8 %all-gather.5.cloned.1.call-start = ((), (), s32[]{:S(2)}) async-start(), calls=%async_computation.1 | async-start | bytes 3981312 | tf_op jit(solution)/shard_map/all_gather | solution.py:234
  81.8 77.3 %all-gather.3.cloned.1.call-start = ((), (), s32[]{:S(2)}) async-start(), calls=%async_computation | async-start | bytes 3981312 | tf_op jit(solution)/shard_map/all_gather | solution.py:234
  146.0 36.0 %collective-permute-start.21 = (bf16[2,6,48,384]{3,2,1,0:T(8,128)(2,1)}, bf16[2,6,48,384]{3,2,1,0:T(8,128)(2,1)S(1)}, u32[]{:S(2)}, u32[]{:S(2)}) collective-permute-start(bf16[2,6,48,384]{3,2,1,0:T(8,128)(2,1)} %get-tuple-element.54), channel_id=1, source_target_pairs={{0,1},{1,0},{2,3},{3,2},{4,5},{5,4},{6,7},{7,6},{8,9},{9,8},{10,11... | collective-permute-start | bytes 1327112 | tf_op jit(solution)/shard_map/ppermute | solution.py:203
  146.5 39.1 %collective-permute-start.22 = (bf16[2,6,48,384]{3,2,1,0:T(8,128)(2,1)}, bf16[2,6,48,384]{3,2,1,0:T(8,128)(2,1)S(1)}, u32[]{:S(2)}, u32[]{:S(2)}) collective-permute-start(bf16[2,6,48,384]{3,2,1,0:T(8,128)(2,1)} %get-tuple-element.55), channel_id=1, source_target_pairs={{0,2},{1,3},{2,0},{3,1},{4,6},{5,7},{6,4},{7,5},{8,10},{9,11},{10,... | collective-permute-start | bytes 1327112 | tf_op jit(solution)/shard_map/ppermute | solution.py:203
  147.9 38.8 %collective-permute-start.23 = (bf16[2,6,48,384]{3,2,1,0:T(8,128)(2,1)}, bf16[2,6,48,384]{3,2,1,0:T(8,128)(2,1)}, u32[]{:S(2)}, u32[]{:S(2)}) collective-permute-start(bf16[2,6,48,384]{3,2,1,0:T(8,128)(2,1)} %get-tuple-element.56), channel_id=1, source_target_pairs={{0,3},{1,2},{2,1},{3,0},{4,7},{5,6},{6,5},{7,4},{8,11},{9,10},{10,... | collective-permute-start | bytes 1327112 | tf_op jit(solution)/shard_map/ppermute | solution.py:203
  150.6 39.4 %collective-permute-start.24 = (bf16[2,6,48,384]{3,2,1,0:T(8,128)(2,1)}, bf16[2,6,48,384]{3,2,1,0:T(8,128)(2,1)}, u32[]{:S(2)}, u32[]{:S(2)}) collective-permute-start(bf16[2,6,48,384]{3,2,1,0:T(8,128)(2,1)} %get-tuple-element.57), channel_id=1, source_target_pairs={{0,4},{1,5},{2,6},{3,7},{4,0},{5,1},{6,2},{7,3},{8,12},{9,13},{10,... | collective-permute-start | bytes 1327112 | tf_op jit(solution)/shard_map/ppermute | solution.py:203
  153.6 39.2 %collective-permute-start.25 = (bf16[2,6,48,384]{3,2,1,0:T(8,128)(2,1)}, bf16[2,6,48,384]{3,2,1,0:T(8,128)(2,1)}, u32[]{:S(2)}, u32[]{:S(2)}) collective-permute-start(bf16[2,6,48,384]{3,2,1,0:T(8,128)(2,1)} %get-tuple-element.58), channel_id=1, source_target_pairs={{0,5},{1,4},{2,7},{3,6},{4,1},{5,0},{6,3},{7,2},{8,13},{9,12},{10,... | collective-permute-start | bytes 1327112 | tf_op jit(solution)/shard_map/ppermute | solution.py:203
  182.8 44.6 %collective-permute-start.26 = (bf16[2,6,48,384]{3,2,1,0:T(8,128)(2,1)}, bf16[2,6,48,384]{3,2,1,0:T(8,128)(2,1)}, u32[]{:S(2)}, u32[]{:S(2)}) collective-permute-start(bf16[2,6,48,384]{3,2,1,0:T(8,128)(2,1)} %get-tuple-element.59), channel_id=1, source_target_pairs={{0,6},{1,7},{2,4},{3,5},{4,2},{5,3},{6,0},{7,1},{8,14},{9,15},{10,... | collective-permute-start | bytes 1327112 | tf_op jit(solution)/shard_map/ppermute | solution.py:203
  186.4 42.6 %collective-permute-start.27 = (bf16[2,6,48,384]{3,2,1,0:T(8,128)(2,1)}, bf16[2,6,48,384]{3,2,1,0:T(8,128)(2,1)}, u32[]{:S(2)}, u32[]{:S(2)}) collective-permute-start(bf16[2,6,48,384]{3,2,1,0:T(8,128)(2,1)} %get-tuple-element.60), channel_id=1, source_target_pairs={{0,7},{1,6},{2,5},{3,4},{4,3},{5,2},{6,1},{7,0},{8,15},{9,14},{10,... | collective-permute-start | bytes 1327112 | tf_op jit(solution)/shard_map/ppermute | solution.py:203
  186.8 43.2 %collective-permute-start.10 = (bf16[2,6,48,384]{3,2,1,0:T(8,128)(2,1)}, bf16[2,6,48,384]{3,2,1,0:T(8,128)(2,1)}, u32[]{:S(2)}, u32[]{:S(2)}) collective-permute-start(bf16[2,6,48,384]{3,2,1,0:T(8,128)(2,1)} %get-tuple-element.41), channel_id=1, source_target_pairs={{0,4},{1,5},{2,6},{3,7},{4,0},{5,1},{6,2},{7,3},{8,12},{9,13},{10,... | collective-permute-start | bytes 1327112 | tf_op jit(solution)/shard_map/ppermute | solution.py:203
  190.0 45.8 %collective-permute-start.11 = (bf16[2,6,48,384]{3,2,1,0:T(8,128)(2,1)}, bf16[2,6,48,384]{3,2,1,0:T(8,128)(2,1)}, u32[]{:S(2)}, u32[]{:S(2)}) collective-permute-start(bf16[2,6,48,384]{3,2,1,0:T(8,128)(2,1)} %copy-done.32), channel_id=1, source_target_pairs={{0,5},{1,4},{2,7},{3,6},{4,1},{5,0},{6,3},{7,2},{8,13},{9,12},{10,... | collective-permute-start | bytes 1327112 | tf_op jit(solution)/shard_map/ppermute | solution.py:203
  192.9 65.7 %collective-permute-start.12 = (bf16[2,6,48,384]{3,2,1,0:T(8,128)(2,1)}, bf16[2,6,48,384]{3,2,1,0:T(8,128)(2,1)}, u32[]{:S(2)}, u32[]{:S(2)}) collective-permute-start(bf16[2,6,48,384]{3,2,1,0:T(8,128)(2,1)} %copy-done.31), channel_id=1, source_target_pairs={{0,6},{1,7},{2,4},{3,5},{4,2},{5,3},{6,0},{7,1},{8,14},{9,15},{10,... | collective-permute-start | bytes 1327112 | tf_op jit(solution)/shard_map/ppermute | solution.py:203
  227.4 32.2 %collective-permute-start.13 = (bf16[2,6,48,384]{3,2,1,0:T(8,128)(2,1)}, bf16[2,6,48,384]{3,2,1,0:T(8,128)(2,1)}, u32[]{:S(2)}, u32[]{:S(2)}) collective-permute-start(bf16[2,6,48,384]{3,2,1,0:T(8,128)(2,1)} %copy-done.30), channel_id=1, source_target_pairs={{0,7},{1,6},{2,5},{3,4},{4,3},{5,2},{6,1},{7,0},{8,15},{9,14},{10,... | collective-permute-start | bytes 1327112 | tf_op jit(solution)/shard_map/ppermute | solution.py:203
  228.9 30.8 %collective-permute-start.7 = (bf16[2,6,48,384]{3,2,1,0:T(8,128)(2,1)}, bf16[2,6,48,384]{3,2,1,0:T(8,128)(2,1)}, u32[]{:S(2)}, u32[]{:S(2)}) collective-permute-start(bf16[2,6,48,384]{3,2,1,0:T(8,128)(2,1)} %copy-done.29), channel_id=1, source_target_pairs={{0,1},{1,0},{2,3},{3,2},{4,5},{5,4},{6,7},{7,6},{8,9},{9,8},{10,11... | collective-permute-start | bytes 1327112 | tf_op jit(solution)/shard_map/ppermute | solution.py:203
  230.0 32.1 %collective-permute-start.8 = (bf16[2,6,48,384]{3,2,1,0:T(8,128)(2,1)}, bf16[2,6,48,384]{3,2,1,0:T(8,128)(2,1)}, u32[]{:S(2)}, u32[]{:S(2)}) collective-permute-start(bf16[2,6,48,384]{3,2,1,0:T(8,128)(2,1)} %copy-done.28), channel_id=1, source_target_pairs={{0,2},{1,3},{2,0},{3,1},{4,6},{5,7},{6,4},{7,5},{8,10},{9,11},{10,... | collective-permute-start | bytes 1327112 | tf_op jit(solution)/shard_map/ppermute | solution.py:203
  259.7 32.5 %collective-permute-start.29 = (bf16[2,6,48,384]{3,2,1,0:T(8,128)(2,1)S(1)}, bf16[2,6,48,384]{3,2,1,0:T(8,128)(2,1)S(1)}, u32[]{:S(2)}, u32[]{:S(2)}) collective-permute-start(bf16[2,6,48,384]{3,2,1,0:T(8,128)(2,1)S(1)} %get-tuple-element.63), channel_id=1, source_target_pairs={{0,2},{1,3},{2,0},{3,1},{4,6},{5,7},{6,4},{7,5},{8,10},{9,11},{10,... | collective-permute-start | bytes 1327112 | tf_op jit(solution)/shard_map/ppermute | solution.py:203
  259.7 35.4 %collective-permute-start.30 = (bf16[2,6,48,384]{3,2,1,0:T(8,128)(2,1)S(1)}, bf16[2,6,48,384]{3,2,1,0:T(8,128)(2,1)S(1)}, u32[]{:S(2)}, u32[]{:S(2)}) collective-permute-start(bf16[2,6,48,384]{3,2,1,0:T(8,128)(2,1)S(1)} %get-tuple-element.64), channel_id=1, source_target_pairs={{0,3},{1,2},{2,1},{3,0},{4,7},{5,6},{6,5},{7,4},{8,11},{9,10},{10,... | collective-permute-start | bytes 1327112 | tf_op jit(solution)/shard_map/ppermute | solution.py:203
  262.1 46.4 %collective-permute-start.31 = (bf16[2,6,48,384]{3,2,1,0:T(8,128)(2,1)S(1)}, bf16[2,6,48,384]{3,2,1,0:T(8,128)(2,1)S(1)}, u32[]{:S(2)}, u32[]{:S(2)}) collective-permute-start(bf16[2,6,48,384]{3,2,1,0:T(8,128)(2,1)S(1)} %get-tuple-element.65), channel_id=1, source_target_pairs={{0,4},{1,5},{2,6},{3,7},{4,0},{5,1},{6,2},{7,3},{8,12},{9,13},{10,... | collective-permute-start | bytes 1327112 | tf_op jit(solution)/shard_map/ppermute | solution.py:203
  264.4 44.8 %collective-permute-start.32 = (bf16[2,6,48,384]{3,2,1,0:T(8,128)(2,1)S(1)}, bf16[2,6,48,384]{3,2,1,0:T(8,128)(2,1)S(1)}, u32[]{:S(2)}, u32[]{:S(2)}) collective-permute-start(bf16[2,6,48,384]{3,2,1,0:T(8,128)(2,1)S(1)} %get-tuple-element.66), channel_id=1, source_target_pairs={{0,5},{1,4},{2,7},{3,6},{4,1},{5,0},{6,3},{7,2},{8,13},{9,12},{10,... | collective-permute-start | bytes 1327112 | tf_op jit(solution)/shard_map/ppermute | solution.py:203
  283.9 34.0 %collective-permute-start.33 = (bf16[2,6,48,384]{3,2,1,0:T(8,128)(2,1)S(1)}, bf16[2,6,48,384]{3,2,1,0:T(8,128)(2,1)S(1)}, u32[]{:S(2)}, u32[]{:S(2)}) collective-permute-start(bf16[2,6,48,384]{3,2,1,0:T(8,128)(2,1)S(1)} %get-tuple-element.67), channel_id=1, source_target_pairs={{0,6},{1,7},{2,4},{3,5},{4,2},{5,3},{6,0},{7,1},{8,14},{9,15},{10,... | collective-permute-start | bytes 1327112 | tf_op jit(solution)/shard_map/ppermute | solution.py:203
  309.9 45.9 %collective-permute-start.16 = (bf16[2,6,48,384]{3,2,1,0:T(8,128)(2,1)}, bf16[2,6,48,384]{3,2,1,0:T(8,128)(2,1)}, u32[]{:S(2)}, u32[]{:S(2)}) collective-permute-start(bf16[2,6,48,384]{3,2,1,0:T(8,128)(2,1)} %get-tuple-element.48), channel_id=1, source_target_pairs={{0,3},{1,2},{2,1},{3,0},{4,7},{5,6},{6,5},{7,4},{8,11},{9,10},{10,... | collective-permute-start | bytes 1327112 | tf_op jit(solution)/shard_map/ppermute | solution.py:203
  318.7 37.1 %collective-permute-start.17 = (bf16[2,6,48,384]{3,2,1,0:T(8,128)(2,1)}, bf16[2,6,48,384]{3,2,1,0:T(8,128)(2,1)}, u32[]{:S(2)}, u32[]{:S(2)}) collective-permute-start(bf16[2,6,48,384]{3,2,1,0:T(8,128)(2,1)} %get-tuple-element.49), channel_id=1, source_target_pairs={{0,4},{1,5},{2,6},{3,7},{4,0},{5,1},{6,2},{7,3},{8,12},{9,13},{10,... | collective-permute-start | bytes 1327112 | tf_op jit(solution)/shard_map/ppermute | solution.py:203
  319.7 36.1 %collective-permute-start.18 = (bf16[2,6,48,384]{3,2,1,0:T(8,128)(2,1)}, bf16[2,6,48,384]{3,2,1,0:T(8,128)(2,1)}, u32[]{:S(2)}, u32[]{:S(2)}) collective-permute-start(bf16[2,6,48,384]{3,2,1,0:T(8,128)(2,1)} %get-tuple-element.50), channel_id=1, source_target_pairs={{0,5},{1,4},{2,7},{3,6},{4,1},{5,0},{6,3},{7,2},{8,13},{9,12},{10,... | collective-permute-start | bytes 1327112 | tf_op jit(solution)/shard_map/ppermute | solution.py:203
  324.3 37.7 %collective-permute-start.19 = (bf16[2,6,48,384]{3,2,1,0:T(8,128)(2,1)}, bf16[2,6,48,384]{3,2,1,0:T(8,128)(2,1)}, u32[]{:S(2)}, u32[]{:S(2)}) collective-permute-start(bf16[2,6,48,384]{3,2,1,0:T(8,128)(2,1)} %get-tuple-element.51), channel_id=1, source_target_pairs={{0,6},{1,7},{2,4},{3,5},{4,2},{5,3},{6,0},{7,1},{8,14},{9,15},{10,... | collective-permute-start | bytes 1327112 | tf_op jit(solution)/shard_map/ppermute | solution.py:203
  (67 other events, 996.2 us)
Sparse Core Ops, SparseCore 0:
  81.9 43.3 all-gather.4
  127.1 31.8 all-gather.2

commit v2 on v1

v2 whole, which is shorter than its diff:
```python
import jax
import jax.numpy as jnp
import numpy as np
from jax import lax
from jax.experimental import pallas as pl
from jax.experimental.pallas import tpu as pltpu
from jax.sharding import PartitionSpec as P

SIDE = 192
PARTS = 8
ROWS = SIDE // PARTS
QUADS = ROWS // 4
DUOS = SIDE // 2
CELLS = SIDE * SIDE
COUL = 160.0
F32 = jnp.float32
BF16 = jnp.bfloat16


def cas_matrix():
    index = np.arange(SIDE, dtype=np.int32)
    phases = (index[:, None] * index[None, :] % SIDE).astype(np.float32) * np.float32(2.0 * np.pi / SIDE)
    return np.cos(phases) + np.sin(phases)


CAS = cas_matrix()
BY_PARITY = np.concatenate([np.arange(0, SIDE, 2), np.arange(1, SIDE, 2)])
Y_TABLE = CAS[:, BY_PARITY]
Y_BACK = CAS[BY_PARITY, :]
X_TABLE = CAS[:, BY_PARITY]
X_BACK = CAS[BY_PARITY, :]


def z_tables():
    gap = np.zeros((64, 256), np.float32)
    space = np.zeros((SIDE, 64), np.float32)
    first = np.concatenate([CAS, space], axis=1)
    second = np.concatenate([CAS[:, :128], space, CAS[:, 128:]], axis=1)
    return np.stack([np.concatenate(part, axis=0) for table in (first, second) for part in ((table, gap), (gap, table))])


Z_TABLES = z_tables()
Z_BACKS = np.swapaxes(Z_TABLES, 1, 2)


def wave(index):
    return jnp.where(index < SIDE // 2, index, index - SIDE).astype(F32)


def coulomb(me):
    shape = (ROWS // 2, SIDE, 384)
    pair = lax.broadcasted_iota(jnp.int32, shape, 0)
    row = lax.broadcasted_iota(jnp.int32, shape, 1)
    col = lax.broadcasted_iota(jnp.int32, shape, 2)
    late = jnp.where(col < 256, col >= 128, col >= 320)
    kz = jnp.where(col < 256, col % 128, 128 + col % 64)
    ky = me * ROWS + pair + jnp.where(late, ROWS // 2, 0)
    mx, my, mz = wave(row), wave(ky), wave(kz)
    norm_sq = mx * mx + my * my + mz * mz
    bounded = jnp.maximum(norm_sq, 1.0)
    return jnp.where(norm_sq > 0.5, COUL / bounded, 0.0) / float(SIDE) ** 3


def dot(left, right):
    return jnp.dot(left, right, preferred_element_type=F32)


def whole(shape):
    return pl.BlockSpec(shape, lambda *_: (0,) * len(shape))


def tiles(lots, rows):
    return jnp.concatenate([lot[rows, :] for lot in lots], axis=1)


def forward_body(target, source, z_tables, y_table, out, *lots):
    chunks = source.shape[0]
    per_chunk = DUOS // chunks

    def form(duo, carry):
        chunk, part = duo // per_chunk, duo % per_chunk
        left = target[:, pl.ds(pl.multiple_of(duo * 384, 128), 384)].astype(F32)
        right = source[chunk, 0, :, pl.ds(pl.multiple_of(part * 384, 128), 384)].astype(F32)
        density = left * right
        for tile, lot in enumerate(lots):
            lot[pl.ds(duo, ROWS, stride=DUOS), :] = density[:, tile * 128 : (tile + 1) * 128]
        return carry

    lax.fori_loop(0, DUOS, form, 0, unroll=4)

    def planes(quad, carry):
        along_y = []
        for pair in range(2):
            halves = []
            for plane in range(2):
                rows = pl.ds(pl.multiple_of((quad * 4 + pair * 2 + plane) * DUOS, DUOS), DUOS)
                density = tiles(lots, rows).astype(BF16)
                even = dot(density[:, :256], z_tables[2 * plane])
                odd = dot(density[:, 128:], z_tables[2 * plane + 1])
                halves.append(jnp.concatenate([even, odd], axis=0))
            low, high = halves
            packed = jnp.concatenate([low[:, :128], high[:, :128], low[:, 128:] + high[:, 128:]], axis=1)
            along_y.append(dot(y_table[...], packed.astype(BF16)))
        for part in range(PARTS):
            rows = slice(part * ROWS, (part + 1) * ROWS)
            out[part, 0, quad] = jnp.concatenate([along_y[0][rows], along_y[1][rows]], axis=0).astype(BF16)
        return carry

    lax.fori_loop(0, QUADS, planes, 0)


def forward(target, sources):
    chunks, pairs = sources.shape[:2]
    return pl.pallas_call(
        forward_body,
        grid=(pairs,),
        in_specs=[
            whole((ROWS, CELLS)),
            pl.BlockSpec((chunks, 1, ROWS, CELLS // chunks), lambda p: (0, p, 0, 0)),
            whole((4, 256, 256)),
            whole((SIDE, SIDE)),
        ],
        out_specs=pl.BlockSpec((PARTS, 1, QUADS, 2 * ROWS, 384), lambda p: (0, p, 0, 0, 0)),
        out_shape=jax.ShapeDtypeStruct((PARTS, pairs, QUADS, 2 * ROWS, 384), BF16),
        scratch_shapes=[pltpu.VMEM((ROWS * DUOS, 128), F32)] * 3,
        compiler_params=pltpu.CompilerParams(vmem_limit_bytes=40 * 2**20),
        cost_estimate=pl.CostEstimate(flops=pairs * 1400 * 10**6, bytes_accessed=pairs * 7 * 10**6, transcendentals=0),
        name="forward_zy",
    )(target, sources, jnp.asarray(Z_TABLES, BF16), jnp.asarray(Y_TABLE, BF16))


def middle_body(pieces, kernel, x_table, x_back, out, head0, head1, tail):
    lots = (head0, head1, tail)
    block = QUADS * 2 * ROWS
    for part in range(PARTS):
        for tile, lot in enumerate(lots):
            lot[part * block : (part + 1) * block] = (
                pieces[part, 0, :, :, tile * 128 : (tile + 1) * 128].astype(F32).reshape(block, 128)
            )
    low = lax.broadcasted_iota(jnp.int32, (DUOS, 128), 1) < 64

    def step(i, carry):
        here = pl.ds(i, DUOS, stride=ROWS)
        there = pl.ds(i + ROWS // 2, DUOS, stride=ROWS)
        tail_a, tail_b = tail[here, :], tail[there, :]
        tail_first = jnp.where(low, tail_a, pltpu.roll(tail_b, 64, 1))
        tail_second = jnp.where(low, pltpu.roll(tail_a, 64, 1), tail_b)
        columns = jnp.concatenate(
            [
                jnp.concatenate([head0[here, :], head0[there, :], tail_first], axis=1),
                jnp.concatenate([head1[here, :], head1[there, :], tail_second], axis=1),
            ],
            axis=0,
        ).astype(BF16)
        spectrum = (kernel[i] * dot(x_table[...], columns)).astype(BF16)
        back = dot(x_back[...], spectrum)
        head0[here, :] = back[:DUOS, :128]
        head1[here, :] = back[DUOS:, :128]
        head0[there, :] = back[:DUOS, 128:256]
        head1[there, :] = back[DUOS:, 128:256]
        first, second = back[:DUOS, 256:], back[DUOS:, 256:]
        tail[here, :] = jnp.where(low, first, pltpu.roll(second, 64, 1))
        tail[there, :] = jnp.where(low, pltpu.roll(first, 64, 1), second)
        return carry

    lax.fori_loop(0, ROWS // 2, step, 0)
    for part in range(PARTS):
        for tile, lot in enumerate(lots):
            out[part, 0, :, :, tile * 128 : (tile + 1) * 128] = (
                lot[part * block : (part + 1) * block].astype(BF16).reshape(QUADS, 2 * ROWS, 128)
            )


def middle(pieces, kernel):
    pairs = pieces.shape[1]
    spec = pl.BlockSpec((PARTS, 1, QUADS, 2 * ROWS, 384), lambda p: (0, p, 0, 0, 0))
    return pl.pallas_call(
        middle_body,
        grid=(pairs,),
        in_specs=[spec, whole(kernel.shape), whole((SIDE, SIDE)), whole((SIDE, SIDE))],
        out_specs=spec,
        out_shape=jax.ShapeDtypeStruct(pieces.shape, BF16),
        scratch_shapes=[pltpu.VMEM((DUOS * ROWS, 128), F32)] * 3,
        compiler_params=pltpu.CompilerParams(vmem_limit_bytes=40 * 2**20),
        cost_estimate=pl.CostEstimate(flops=pairs * 1400 * 10**6, bytes_accessed=pairs * 7 * 10**6, transcendentals=0),
        name="middle_x",
    )(pieces, kernel, jnp.asarray(X_TABLE, BF16), jnp.asarray(X_BACK, BF16))


def backward_body(pieces, source, *refs):
    (total, y_table, z_tables, out), lots = ((None,) + refs[:3], refs[3:]) if len(refs) == 6 else (refs[:4], refs[4:])
    chunks = source.shape[0]
    per_chunk = DUOS // chunks

    @pl.when(pl.program_id(0) == 0)
    def _():
        if total is None:
            out[...] = jnp.zeros(out.shape, F32)
        else:
            out[...] = total[...]

    def planes(quad, carry):
        parts = [pieces[part, 0, quad].astype(F32) for part in range(PARTS)]
        for pair in range(2):
            stack = jnp.concatenate([part[pair * ROWS : (pair + 1) * ROWS] for part in parts], axis=0)
            fields = dot(y_table[...], stack.astype(BF16)).astype(BF16)
            for plane in range(2):
                lanes = fields[:, 128:] if plane else jnp.concatenate([fields[:, :128], fields[:, 256:]], axis=1)
                even = dot(lanes[:DUOS], z_tables[2 * plane])
                odd = dot(lanes[DUOS:], z_tables[2 * plane + 1])
                rows = pl.ds(pl.multiple_of((quad * 4 + pair * 2 + plane) * DUOS, DUOS), DUOS)
                lots[0][rows, :] = even[:, :128]
                lots[1][rows, :] = even[:, 128:] + odd[:, :128]
                lots[2][rows, :] = odd[:, 128:]
        return carry

    lax.fori_loop(0, QUADS, planes, 0)

    def gather(duo, carry):
        chunk, part = duo // per_chunk, duo % per_chunk
        potential = tiles(lots, pl.ds(duo, ROWS, stride=DUOS))
        here = pl.ds(pl.multiple_of(duo * 384, 128), 384)
        right = source[chunk, 0, :, pl.ds(pl.multiple_of(part * 384, 128), 384)].astype(F32)
        out[:, here] = out[:, here] - potential * right
        return carry

    lax.fori_loop(0, DUOS, gather, 0, unroll=4)


def backward(pieces, sources, total):
    chunks, pairs = sources.shape[:2]
    return pl.pallas_call(
        backward_body,
        grid=(pairs,),
        in_specs=[
            pl.BlockSpec((PARTS, 1, QUADS, 2 * ROWS, 384), lambda p: (0, p, 0, 0, 0)),
            pl.BlockSpec((chunks, 1, ROWS, CELLS // chunks), lambda p: (0, p, 0, 0)),
        ]
        + [whole((ROWS, CELLS))] * (total is not None)
        + [whole((SIDE, SIDE)), whole((4, 256, 256))],
        out_specs=whole((ROWS, CELLS)),
        out_shape=jax.ShapeDtypeStruct((ROWS, CELLS), F32),
        scratch_shapes=[pltpu.VMEM((ROWS * DUOS, 128), F32)] * 3,
        compiler_params=pltpu.CompilerParams(vmem_limit_bytes=48 * 2**20),
        cost_estimate=pl.CostEstimate(flops=pairs * 1400 * 10**6, bytes_accessed=pairs * 7 * 10**6, transcendentals=0),
        name="backward_yz",
    )(pieces, sources, *([] if total is None else [total]), jnp.asarray(Y_BACK, BF16), jnp.asarray(Z_BACKS, BF16))


def exchange(pieces):
    return lax.all_to_all(pieces, "grid", 0, 0, tiled=True)


def band_of(z_hi, x, core):
    return z_hi * 8 + x * 2 + core


def spread(orbitals):
    band = lax.axis_index("band")
    z_hi, x = band // 8, (band // 2) % 4
    core = band % 2
    cut = CELLS // 4
    mine = jnp.where(x == 0, orbitals[:, :cut], jnp.zeros((), BF16))
    for step in range(1, 4):
        pairs = [(band_of(z, 0, 0), band_of(z, step, 0)) for z in (0, 2)]
        mine = mine + lax.ppermute(orbitals[:, step * cut : (step + 1) * cut], "band", pairs)
    swap = [(band_of(z, i, 0), band_of(z, i, 1)) for z in (0, 2) for i in range(4)]
    other = lax.ppermute(mine[:, cut // 2 :], "band", swap)
    mine = jnp.where(core == 0, mine[:, : cut // 2], other)
    got = []
    for moves in (((0, 1), (2, 3)), ((0, 3), (2, 1)), ((0, 2), (2, 0))):
        pairs = [(band_of(a, i, c), band_of(b, i, c)) for a, b in moves for i in range(4) for c in range(2)]
        got.append(lax.ppermute(mine, "band", pairs))
    near, far, cross = got
    from_first = jnp.where(z_hi == 0, mine, jnp.where(z_hi == 1, near, jnp.where(z_hi == 2, cross, far)))
    from_second = jnp.where(z_hi == 2, mine, jnp.where(z_hi == 3, near, jnp.where(z_hi == 0, cross, far)))
    groups = [[8 * k + i for i in range(8)] for k in range(4)]
    return lax.all_gather(jnp.stack([from_first, from_second]), "band", axis=0, axis_index_groups=groups)


def local(orbitals):
    kernel = coulomb(lax.axis_index("grid"))
    batches = [spread(orbitals[p]) for p in range(2)]
    backs = []
    for sources in batches:
        pieces = exchange(forward(orbitals[0], sources))
        backs.append(exchange(middle(pieces, kernel)))
    total = None
    for pieces, sources in zip(backs, batches):
        total = backward(pieces, sources, total)
    return total[None]


def solution(mesh):
    return jax.shard_map(
        local,
        mesh=mesh,
        in_specs=(P("band", "grid", None),),
        out_specs=P("band", "grid", None),
        check_vma=False,
    )
```

time: 388 us -> 332 us (0.86)
  local copies, waits for them, and re-layouts: 75.7 us -> 31.5 us
  Pallas kernels: 64.2 us -> 98.6 us
  waiting for transfers between devices: 144 us -> 115 us
  other arithmetic: 22.1 us -> 8.24 us
    ppermute x32 -> x8, waiting for transfers between devices: 93.5 us -> 12.9 us  [the longest x6 11.1 us: spread(): lax.ppermute(orbitals[:, step * cut:(step + 1) * cut], 'band', pairs)]
    all_to_all x0 -> x4, waiting for transfers between devices: none -> 72.7 us  [exchange(): return lax.all_to_all(pieces, 'grid', 0, 0, tiled=True)]
    pallas_call x6, Pallas kernels: 64.2 us -> 98.6 us  [the longest x2 35.8 us: backward(): pl.pallas_call(backward_body, grid=(pairs,), in_specs=[pl.BlockSpec((PART...]
    reshape x6 -> x0, local copies, waits for them, and re-layouts: 32.8 us -> none  [the longest x4 21.8 us: spread(): g.reshape(8, 2, ROWS, ROWS, SIDE)]
    ppermute x32 -> x8, starting transfers between devices: 52.1 us -> 20.2 us  [the longest x6 17 us: spread(): lax.ppermute(orbitals[:, step * cut:(step + 1) * cut], 'band', pairs)]
    all_to_all x0 -> x4, starting transfers between devices: none -> 21.8 us  [exchange(): return lax.all_to_all(pieces, 'grid', 0, 0, tiled=True)]
    all_gather x2, waiting for transfers between devices: 32.1 us -> 12.4 us  [spread(): lax.all_gather(jnp.stack([from_first, from_second]), 'band', axis=0, axis...]
    ppermute x3 -> x6, starting transfers between devices: 12.3 us -> 19.1 us  [spread(): got.append(lax.ppermute(mine, 'band', pairs))]
  transfers between devices with their start and end apart: 37 -> 20, of which waited for: 12 -> 17; matrix products, arithmetic and copies ran while one was open for 13% -> 1% of each run, Pallas kernels for 15% -> 24%
where the time goes in v2:
time: 332 us; the launch traced here: 328 us
  waiting for transfers between devices  115 us (35%)
  Pallas kernels  98.6 us (30%)
  starting transfers between devices  61.1 us (18%)
  local copies, waits for them, and re-layouts  31.5 us (9%)
  between operations  13.7 us (4%)
  other arithmetic  8.24 us (2%)
    all_to_all x4, waiting for transfers between devices, exchange(): return lax.all_to_all(pieces, 'grid', 0, 0, tiled=True)  72.7 us
    pallas_call x2, Pallas kernels, backward(): pl.pallas_call(backward_body, grid=(pairs,), in_specs=[pl.BlockSpec((PART...  35.8 us
    pallas_call x2, Pallas kernels, forward(): pl.pallas_call(forward_body, grid=(pairs,), in_specs=[whole((ROWS, CELLS)...  33.4 us
    pallas_call x2, Pallas kernels, middle(): pl.pallas_call(middle_body, grid=(pairs,), in_specs=[spec, whole(kernel.s...  29.4 us
    unnamed x50, local copies, waits for them, and re-layouts  27.3 us
    all_to_all x4, starting transfers between devices, exchange(): return lax.all_to_all(pieces, 'grid', 0, 0, tiled=True)  21.8 us
    ppermute x6, starting transfers between devices, spread(): got.append(lax.ppermute(mine, 'band', pairs))  19.1 us
    ppermute x6, waiting for transfers between devices, spread(): got.append(lax.ppermute(mine, 'band', pairs))  17.1 us
  transfers between devices with their start and end apart: 20, of which 17 were waited for; matrix products, arithmetic and copies ran while one was open for 1% of the time, Pallas kernels for 24%

profile of v2, /device:TPU:32, one launch (start us, length us, event | category | flops | bytes accessed | tf_op | source)
XLA Modules:
  0.0 328.4 jit_solution(5971643413729158188)
XLA Ops:
  10.0 4.2 %collective-permute-start.7 = (bf16[24,9216]{1,0:T(8,128)(2,1)}, bf16[24,9216]{1,0:T(8,128)(2,1)}, u32[]{:S(2)}, u32[]{:S(2)}) collective-permute-start(bf16[24,9216]{1,0:T(8,128)(2,1)} %get-tuple-element.7), channel_id=1, source_target_pairs={{0,16},{128,144},{1,17},{129,145},{2,18},{130,146},{3,19},{131,147... | collective-permute-start | bytes 1327112 | tf_op jit(solution)/shard_map/ppermute | solution.py:266
  19.5 4.7 %collective-permute-done.8 = bf16[24,9216]{1,0:T(8,128)(2,1)} collective-permute-done((bf16[24,9216]{1,0:T(8,128)(2,1)}, bf16[24,9216]{1,0:T(8,128)(2,1)}, u32[]{:S(2)}, u32[]{:S(2)}) %collective-permute-start.8) | collective-permute-done | bytes 442400 | tf_op jit(solution)/shard_map/ppermute | solution.py:266
  33.7 8.2 %collective-permute-start.12 = (bf16[24,4608]{1,0:T(8,128)(2,1)}, bf16[24,4608]{1,0:T(8,128)(2,1)}, u32[]{:S(2)}, u32[]{:S(2)}) collective-permute-start(bf16[24,4608]{1,0:T(8,128)(2,1)} %slice_select_fusion.2), channel_id=1, source_target_pairs={{0,128},{8,136},{16,144},{24,152},{32,160},{40,168},{48,176},{56,1... | collective-permute-start | bytes 663560 | tf_op jit(solution)/shard_map/ppermute | solution.py:273
  43.8 4.7 %collective-permute-done.12 = bf16[24,4608]{1,0:T(8,128)(2,1)} collective-permute-done((bf16[24,4608]{1,0:T(8,128)(2,1)}, bf16[24,4608]{1,0:T(8,128)(2,1)}, u32[]{:S(2)}, u32[]{:S(2)}) %collective-permute-start.12) | collective-permute-done | bytes 221216 | tf_op jit(solution)/shard_map/ppermute | solution.py:273
  56.1 5.0 %collective-permute-start.1 = (bf16[24,9216]{1,0:T(8,128)(2,1)S(1)}, bf16[24,9216]{1,0:T(8,128)(2,1)S(1)}, u32[]{:S(2)}, u32[]{:S(2)}) collective-permute-start(bf16[24,9216]{1,0:T(8,128)(2,1)S(1)} %get-tuple-element.12), channel_id=1, source_target_pairs={{0,32},{128,160},{1,33},{129,161},{2,34},{130,162},{3,35},{131,163... | collective-permute-start | bytes 1327112 | tf_op jit(solution)/shard_map/ppermute | solution.py:266
  62.5 4.4 %collective-permute-done.1 = bf16[24,9216]{1,0:T(8,128)(2,1)S(1)} collective-permute-done((bf16[24,9216]{1,0:T(8,128)(2,1)S(1)}, bf16[24,9216]{1,0:T(8,128)(2,1)S(1)}, u32[]{:S(2)}, u32[]{:S(2)}) %collective-permute-start.1) | collective-permute-done | bytes 442400 | tf_op jit(solution)/shard_map/ppermute | solution.py:266
  73.1 4.3 %collective-permute-start.5 = (bf16[24,4608]{1,0:T(8,128)(2,1)S(1)}, bf16[24,4608]{1,0:T(8,128)(2,1)S(1)}, u32[]{:S(2)}, u32[]{:S(2)}) collective-permute-start(bf16[24,4608]{1,0:T(8,128)(2,1)S(1)} %slice_select_fusion.3), channel_id=1, source_target_pairs={{0,128},{8,136},{16,144},{24,152},{32,160},{40,168},{48,176},{56,1... | collective-permute-start | bytes 663560 | tf_op jit(solution)/shard_map/ppermute | solution.py:273
  78.7 8.4 %collective-permute-done.5 = bf16[24,4608]{1,0:T(8,128)(2,1)S(1)} collective-permute-done((bf16[24,4608]{1,0:T(8,128)(2,1)S(1)}, bf16[24,4608]{1,0:T(8,128)(2,1)S(1)}, u32[]{:S(2)}, u32[]{:S(2)}) %collective-permute-start.5) | collective-permute-done | bytes 221216 | tf_op jit(solution)/shard_map/ppermute | solution.py:273
  88.3 5.0 %all-gather.7.cloned.1.call-done = bf16[16,24,4608]{2,1,0:T(8,128)(2,1)} async-done(((bf16[2,24,4608]{2,1,0:T(8,128)(2,1)}), bf16[16,24,4608]{2,1,0:T(8,128)(2,1)}) %all-gather.7.cloned.1.call-update) | async-done | bytes 3538960 | tf_op jit(solution)/shard_map/all_gather | solution.py:278
  95.3 16.7 %forward_zy.3 = bf16[8,2,6,48,384]{4,3,2,1,0:T(8,128)(2,1)S(1)} custom-call(bf16[24,36864]{1,0:T(8,128)(2,1)S(1)} %get-tuple-element.6.target, bf16[8,2,24,4608]{3,2,1,0:T(8,128)(2,1)S(1)} %bitcast.18, bf16[4,256,256]{2,1,0:T(8,128)(2,1)S(1)} %copy-done.21, bf16[192,192]{1,0:T(8,128)(2,1)S(1)} %copy-done.17), custom_call_target="tpu_custom_call" | custom-call | flops 2800000000 | bytes 14000000 | tf_op jit(solution)/shard_map/forward_zy/pallas_call | solution.py:114
  113.9 5.8 %all-to-all-start.2 = ((bf16[8,2,6,48,384]{4,3,2,1,0:T(8,128)(2,1)}), bf16[8,2,6,48,384]{4,3,2,1,0:T(8,128)(2,1)S(1)}, u32[]{:S(2)}, u32[]{:S(2)}) async-start(bf16[8,2,6,48,384]{4,3,2,1,0:T(8,128)(2,1)} %copy-done.10), calls=%async_computation.2 | async-start | bytes 7077888 | tf_op jit(solution)/shard_map/all_to_all | solution.py:251
  119.7 7.4 %all-gather.5.cloned.1.call-done = bf16[16,24,4608]{2,1,0:T(8,128)(2,1)} async-done(((bf16[2,24,4608]{2,1,0:T(8,128)(2,1)}), bf16[16,24,4608]{2,1,0:T(8,128)(2,1)}) %all-gather.5.cloned.1.call-update) | async-done | bytes 3538960 | tf_op jit(solution)/shard_map/all_gather | solution.py:278
  132.5 16.7 %forward_zy.2 = bf16[8,2,6,48,384]{4,3,2,1,0:T(8,128)(2,1)S(1)} custom-call(bf16[24,36864]{1,0:T(8,128)(2,1)S(1)} %copy-done.6, bf16[8,2,24,4608]{3,2,1,0:T(8,128)(2,1)S(1)} %bitcast.16, bf16[4,256,256]{2,1,0:T(8,128)(2,1)S(1)} %copy-done.22, bf16[192,192]{1,0:T(8,128)(2,1)S(1)} %copy-done.18), custom_call_target="tpu_custom_call" | custom-call | flops 2800000000 | bytes 14000000 | tf_op jit(solution)/shard_map/forward_zy/pallas_call | solution.py:114
  151.0 10.3 %all-to-all-done.2.pieces = bf16[8,2,6,48,384]{4,3,2,1,0:T(8,128)(2,1)S(1)} async-done(((bf16[8,2,6,48,384]{4,3,2,1,0:T(8,128)(2,1)}), bf16[8,2,6,48,384]{4,3,2,1,0:T(8,128)(2,1)S(1)}, u32[]{:S(2)}, u32[]{:S(2)}) %all-to-all-start.2) | async-done | bytes 3538976 | tf_op jit(solution)/shard_map/all_to_all | solution.py:251
  163.1 5.6 %all-to-all-start = ((bf16[8,2,6,48,384]{4,3,2,1,0:T(8,128)(2,1)}), bf16[8,2,6,48,384]{4,3,2,1,0:T(8,128)(2,1)}, u32[]{:S(2)}, u32[]{:S(2)}) async-start(bf16[8,2,6,48,384]{4,3,2,1,0:T(8,128)(2,1)} %copy-done.9), calls=%async_computation | async-start | bytes 7077888 | tf_op jit(solution)/shard_map/all_to_all | solution.py:251
  172.6 14.2 %middle_x.3 = bf16[8,2,6,48,384]{4,3,2,1,0:T(8,128)(2,1)S(1)} custom-call(bf16[8,2,6,48,384]{4,3,2,1,0:T(8,128)(2,1)S(1)} %copy-done.2, f32[12,192,384]{2,1,0:T(8,128)S(1)} %select_multiply_fusion.kernel, bf16[192,192]{1,0:T(8,128)(2,1)S(1)} %copy-done.19, bf16[192,192]{1,0:T(8,128)(2,1)S(1)} %copy-done.13), custom_call_target="tpu_custom_call" | custom-call | flops 2800000000 | bytes 14000000 | tf_op jit(solution)/shard_map/middle_x/pallas_call | solution.py:177
  188.5 21.2 %all-to-all-done.pieces = bf16[8,2,6,48,384]{4,3,2,1,0:T(8,128)(2,1)} async-done(((bf16[8,2,6,48,384]{4,3,2,1,0:T(8,128)(2,1)}), bf16[8,2,6,48,384]{4,3,2,1,0:T(8,128)(2,1)}, u32[]{:S(2)}, u32[]{:S(2)}) %all-to-all-start) | async-done | bytes 3538976 | tf_op jit(solution)/shard_map/all_to_all | solution.py:251
  209.7 5.6 %all-to-all-start.3 = ((bf16[8,2,6,48,384]{4,3,2,1,0:T(8,128)(2,1)}), bf16[8,2,6,48,384]{4,3,2,1,0:T(8,128)(2,1)}, u32[]{:S(2)}, u32[]{:S(2)}) async-start(bf16[8,2,6,48,384]{4,3,2,1,0:T(8,128)(2,1)} %copy-done.4), calls=%async_computation.3 | async-start | bytes 7077888 | tf_op jit(solution)/shard_map/all_to_all | solution.py:251
  217.0 15.3 %middle_x.2 = bf16[8,2,6,48,384]{4,3,2,1,0:T(8,128)(2,1)S(1)} custom-call(bf16[8,2,6,48,384]{4,3,2,1,0:T(8,128)(2,1)} %all-to-all-done.pieces, f32[12,192,384]{2,1,0:T(8,128)S(1)} %select_multiply_fusion.kernel, bf16[192,192]{1,0:T(8,128)(2,1)S(1)} %copy-done.20, bf16[192,192]{1,0:T(8,128)(2,1)S(1)} %copy-done.14), custom_call_target="tpu_custom_call" | custom-call | flops 2800000000 | bytes 14000000 | tf_op jit(solution)/shard_map/middle_x/pallas_call | solution.py:177
  234.1 21.1 %all-to-all-done.3.pieces = bf16[8,2,6,48,384]{4,3,2,1,0:T(8,128)(2,1)} async-done(((bf16[8,2,6,48,384]{4,3,2,1,0:T(8,128)(2,1)}), bf16[8,2,6,48,384]{4,3,2,1,0:T(8,128)(2,1)}, u32[]{:S(2)}, u32[]{:S(2)}) %all-to-all-start.3) | async-done | bytes 3538976 | tf_op jit(solution)/shard_map/all_to_all | solution.py:251
  255.2 4.8 %all-to-all-start.1 = ((bf16[8,2,6,48,384]{4,3,2,1,0:T(8,128)(2,1)}), bf16[8,2,6,48,384]{4,3,2,1,0:T(8,128)(2,1)S(1)}, u32[]{:S(2)}, u32[]{:S(2)}) async-start(bf16[8,2,6,48,384]{4,3,2,1,0:T(8,128)(2,1)} %copy-done.3), calls=%async_computation.1 | async-start | bytes 7077888 | tf_op jit(solution)/shard_map/all_to_all | solution.py:251
  262.0 16.7 %backward_yz.2.refs_0_ = f32[24,36864]{1,0:T(8,128)S(1)} custom-call(bf16[8,2,6,48,384]{4,3,2,1,0:T(8,128)(2,1)} %all-to-all-done.3.pieces, bf16[8,2,24,4608]{3,2,1,0:T(8,128)(2,1)} %bitcast.17, bf16[192,192]{1,0:T(8,128)(2,1)S(1)} %copy-done.15, bf16[4,256,256]{2,1,0:T(8,128)(2,1)S(1)} %copy-done.11), custom_call_target="tpu_custom_call" | custom-call | flops 2800000000 | bytes 14000000 | tf_op jit(solution)/shard_map/backward_yz/pallas_call | solution.py:232
  280.4 20.1 %all-to-all-done.1.pieces = bf16[8,2,6,48,384]{4,3,2,1,0:T(8,128)(2,1)S(1)} async-done(((bf16[8,2,6,48,384]{4,3,2,1,0:T(8,128)(2,1)}), bf16[8,2,6,48,384]{4,3,2,1,0:T(8,128)(2,1)S(1)}, u32[]{:S(2)}, u32[]{:S(2)}) %all-to-all-start.1) | async-done | bytes 3538976 | tf_op jit(solution)/shard_map/all_to_all | solution.py:251
  302.5 19.1 %backward_yz.3 = f32[24,36864]{1,0:T(8,128)} custom-call(bf16[8,2,6,48,384]{4,3,2,1,0:T(8,128)(2,1)S(1)} %all-to-all-done.1.pieces, bf16[8,2,24,4608]{3,2,1,0:T(8,128)(2,1)} %bitcast.15, f32[24,36864]{1,0:T(8,128)} %copy-done, bf16[192,192]{1,0:T(8,128)(2,1)S(1)} %copy-done.16, bf16[4,256,256]{2,1,0:T(8,128)(2,1)S(1)} %copy-done.12), custom_call_target="tpu_custom_call" | custom-call | flops 2800000000 | bytes 14000000 | tf_op jit(solution)/shard_map/backward_yz/pallas_call | solution.py:232
  (96 shorter events, 65.2 us)
Async XLA Ops:
  6.5 86.7 %all-gather.7.cloned.1.call-start = ((), (), s32[]{:S(2)}) async-start(), calls=%async_computation.5 | async-start | bytes 3981312 | tf_op jit(solution)/shard_map/all_gather | solution.py:278
  8.8 45.7 %copy-start.23 = (bf16[24,36864]{1,0:T(8,128)(2,1)}, bf16[24,36864]{1,0:T(8,128)(2,1)S(1)}, u32[]{:S(2)}) copy-start(bf16[24,36864]{1,0:T(8,128)(2,1)S(1)} %get-tuple-element.5) | copy-start | bytes 5308420
  8.8 84.5 %copy-start.5 = (bf16[24,36864]{1,0:T(8,128)(2,1)}, bf16[24,36864]{1,0:T(8,128)(2,1)S(1)}, u32[]{:S(2)}) copy-start(bf16[24,36864]{1,0:T(8,128)(2,1)S(1)} %get-tuple-element.6.target) | copy-start | bytes 5308420
  10.0 9.5 %collective-permute-start.7 = (bf16[24,9216]{1,0:T(8,128)(2,1)}, bf16[24,9216]{1,0:T(8,128)(2,1)}, u32[]{:S(2)}, u32[]{:S(2)}) collective-permute-start(bf16[24,9216]{1,0:T(8,128)(2,1)} %get-tuple-element.7), channel_id=1, source_target_pairs={{0,16},{128,144},{1,17},{129,145},{2,18},{130,146},{3,19},{131,147... | collective-permute-start | bytes 1327112 | tf_op jit(solution)/shard_map/ppermute | solution.py:266
  14.1 10.1 %collective-permute-start.8 = (bf16[24,9216]{1,0:T(8,128)(2,1)}, bf16[24,9216]{1,0:T(8,128)(2,1)}, u32[]{:S(2)}, u32[]{:S(2)}) collective-permute-start(bf16[24,9216]{1,0:T(8,128)(2,1)} %get-tuple-element.9), channel_id=1, source_target_pairs={{0,32},{128,160},{1,33},{129,161},{2,34},{130,162},{3,35},{131,163... | collective-permute-start | bytes 1327112 | tf_op jit(solution)/shard_map/ppermute | solution.py:266
  17.1 7.4 %collective-permute-start.9 = (bf16[24,9216]{1,0:T(8,128)(2,1)}, bf16[24,9216]{1,0:T(8,128)(2,1)}, u32[]{:S(2)}, u32[]{:S(2)}) collective-permute-start(bf16[24,9216]{1,0:T(8,128)(2,1)} %get-tuple-element.8), channel_id=1, source_target_pairs={{0,48},{128,176},{1,49},{129,177},{2,50},{130,178},{3,51},{131,179... | collective-permute-start | bytes 1327112 | tf_op jit(solution)/shard_map/ppermute | solution.py:266
  27.3 2.7 collective-permute-start.10
  31.7 12.2 %collective-permute-start.11 = (bf16[24,4608]{1,0:T(8,128)(2,1)}, bf16[24,4608]{1,0:T(8,128)(2,1)}, u32[]{:S(2)}, u32[]{:S(2)}) collective-permute-start(bf16[24,4608]{1,0:T(8,128)(2,1)} %slice_select_fusion.2), channel_id=1, source_target_pairs={{0,64},{8,72},{16,80},{24,88},{32,96},{40,104},{48,112},{56,120},{... | collective-permute-start | bytes 663560 | tf_op jit(solution)/shard_map/ppermute | solution.py:273
  33.7 14.9 %collective-permute-start.12 = (bf16[24,4608]{1,0:T(8,128)(2,1)}, bf16[24,4608]{1,0:T(8,128)(2,1)}, u32[]{:S(2)}, u32[]{:S(2)}) collective-permute-start(bf16[24,4608]{1,0:T(8,128)(2,1)} %slice_select_fusion.2), channel_id=1, source_target_pairs={{0,128},{8,136},{16,144},{24,152},{32,160},{40,168},{48,176},{56,1... | collective-permute-start | bytes 663560 | tf_op jit(solution)/shard_map/ppermute | solution.py:273
  41.8 10.4 %collective-permute-start.13 = (bf16[24,4608]{1,0:T(8,128)(2,1)}, bf16[24,4608]{1,0:T(8,128)(2,1)}, u32[]{:S(2)}, u32[]{:S(2)}) collective-permute-start(bf16[24,4608]{1,0:T(8,128)(2,1)} %slice_select_fusion.2), channel_id=1, source_target_pairs={{0,192},{8,200},{16,208},{24,216},{32,224},{40,232},{48,240},{56,2... | collective-permute-start | bytes 663560 | tf_op jit(solution)/shard_map/ppermute | solution.py:273
  54.5 72.6 %all-gather.5.cloned.1.call-start = ((), (), s32[]{:S(2)}) async-start(), calls=%async_computation.4 | async-start | bytes 3981312 | tf_op jit(solution)/shard_map/all_gather | solution.py:278
  54.6 38.7 %copy-start.17 = (bf16[192,192]{1,0:T(8,128)(2,1)S(1)}, bf16[192,192]{1,0:T(8,128)(2,1)}, u32[]{:S(2)}) copy-start(bf16[192,192]{1,0:T(8,128)(2,1)} %constant.129.clone.y_table.x_table) | copy-start | bytes 221188
  54.6 38.7 %copy-start.21 = (bf16[4,256,256]{2,1,0:T(8,128)(2,1)S(1)}, bf16[4,256,256]{2,1,0:T(8,128)(2,1)}, u32[]{:S(2)}) copy-start(bf16[4,256,256]{2,1,0:T(8,128)(2,1)} %constant.128.clone.z_tables) | copy-start | bytes 1572868
  54.6 7.8 %collective-permute-start = (bf16[24,9216]{1,0:T(8,128)(2,1)S(1)}, bf16[24,9216]{1,0:T(8,128)(2,1)S(1)}, u32[]{:S(2)}, u32[]{:S(2)}) collective-permute-start(bf16[24,9216]{1,0:T(8,128)(2,1)S(1)} %get-tuple-element.10), channel_id=1, source_target_pairs={{0,16},{128,144},{1,17},{129,145},{2,18},{130,146},{3,19},{131,147... | collective-permute-start | bytes 1327112 | tf_op jit(solution)/shard_map/ppermute | solution.py:266
  56.1 10.8 %collective-permute-start.1 = (bf16[24,9216]{1,0:T(8,128)(2,1)S(1)}, bf16[24,9216]{1,0:T(8,128)(2,1)S(1)}, u32[]{:S(2)}, u32[]{:S(2)}) collective-permute-start(bf16[24,9216]{1,0:T(8,128)(2,1)S(1)} %get-tuple-element.12), channel_id=1, source_target_pairs={{0,32},{128,160},{1,33},{129,161},{2,34},{130,162},{3,35},{131,163... | collective-permute-start | bytes 1327112 | tf_op jit(solution)/shard_map/ppermute | solution.py:266
  61.1 7.1 %collective-permute-start.2 = (bf16[24,9216]{1,0:T(8,128)(2,1)S(1)}, bf16[24,9216]{1,0:T(8,128)(2,1)S(1)}, u32[]{:S(2)}, u32[]{:S(2)}) collective-permute-start(bf16[24,9216]{1,0:T(8,128)(2,1)S(1)} %get-tuple-element.11), channel_id=1, source_target_pairs={{0,48},{128,176},{1,49},{129,177},{2,50},{130,178},{3,51},{131,179... | collective-permute-start | bytes 1327112 | tf_op jit(solution)/shard_map/ppermute | solution.py:266
  69.3 2.4 collective-permute-start.3
  71.8 7.0 %collective-permute-start.4 = (bf16[24,4608]{1,0:T(8,128)(2,1)S(1)}, bf16[24,4608]{1,0:T(8,128)(2,1)S(1)}, u32[]{:S(2)}, u32[]{:S(2)}) collective-permute-start(bf16[24,4608]{1,0:T(8,128)(2,1)S(1)} %slice_select_fusion.3), channel_id=1, source_target_pairs={{0,64},{8,72},{16,80},{24,88},{32,96},{40,104},{48,112},{56,120},{... | collective-permute-start | bytes 663560 | tf_op jit(solution)/shard_map/ppermute | solution.py:273
  73.1 14.1 %collective-permute-start.5 = (bf16[24,4608]{1,0:T(8,128)(2,1)S(1)}, bf16[24,4608]{1,0:T(8,128)(2,1)S(1)}, u32[]{:S(2)}, u32[]{:S(2)}) collective-permute-start(bf16[24,4608]{1,0:T(8,128)(2,1)S(1)} %slice_select_fusion.3), channel_id=1, source_target_pairs={{0,128},{8,136},{16,144},{24,152},{32,160},{40,168},{48,176},{56,1... | collective-permute-start | bytes 663560 | tf_op jit(solution)/shard_map/ppermute | solution.py:273
  77.4 10.0 %collective-permute-start.6 = (bf16[24,4608]{1,0:T(8,128)(2,1)S(1)}, bf16[24,4608]{1,0:T(8,128)(2,1)S(1)}, u32[]{:S(2)}, u32[]{:S(2)}) collective-permute-start(bf16[24,4608]{1,0:T(8,128)(2,1)S(1)} %slice_select_fusion.3), channel_id=1, source_target_pairs={{0,192},{8,200},{16,208},{24,216},{32,224},{40,232},{48,240},{56,2... | collective-permute-start | bytes 663560 | tf_op jit(solution)/shard_map/ppermute | solution.py:273
  113.9 47.4 %all-to-all-start.2 = ((bf16[8,2,6,48,384]{4,3,2,1,0:T(8,128)(2,1)}), bf16[8,2,6,48,384]{4,3,2,1,0:T(8,128)(2,1)S(1)}, u32[]{:S(2)}, u32[]{:S(2)}) async-start(bf16[8,2,6,48,384]{4,3,2,1,0:T(8,128)(2,1)} %copy-done.10), calls=%async_computation.2 | async-start | bytes 7077888 | tf_op jit(solution)/shard_map/all_to_all | solution.py:251
  163.1 46.5 %all-to-all-start = ((bf16[8,2,6,48,384]{4,3,2,1,0:T(8,128)(2,1)}), bf16[8,2,6,48,384]{4,3,2,1,0:T(8,128)(2,1)}, u32[]{:S(2)}, u32[]{:S(2)}) async-start(bf16[8,2,6,48,384]{4,3,2,1,0:T(8,128)(2,1)} %copy-done.9), calls=%async_computation | async-start | bytes 7077888 | tf_op jit(solution)/shard_map/all_to_all | solution.py:251
  209.7 45.6 %all-to-all-start.3 = ((bf16[8,2,6,48,384]{4,3,2,1,0:T(8,128)(2,1)}), bf16[8,2,6,48,384]{4,3,2,1,0:T(8,128)(2,1)}, u32[]{:S(2)}, u32[]{:S(2)}) async-start(bf16[8,2,6,48,384]{4,3,2,1,0:T(8,128)(2,1)} %copy-done.4), calls=%async_computation.3 | async-start | bytes 7077888 | tf_op jit(solution)/shard_map/all_to_all | solution.py:251
  255.2 45.3 %all-to-all-start.1 = ((bf16[8,2,6,48,384]{4,3,2,1,0:T(8,128)(2,1)}), bf16[8,2,6,48,384]{4,3,2,1,0:T(8,128)(2,1)S(1)}, u32[]{:S(2)}, u32[]{:S(2)}) async-start(bf16[8,2,6,48,384]{4,3,2,1,0:T(8,128)(2,1)} %copy-done.3), calls=%async_computation.1 | async-start | bytes 7077888 | tf_op jit(solution)/shard_map/all_to_all | solution.py:251
  (21 other events, 28.5 us)
Sparse Core Ops, SparseCore 0:
  54.6 38.6 all-gather.6
  95.1 31.9 all-gather.4

commit v3 on v2

v3 whole, which is shorter than its diff:
```python
import jax
import jax.numpy as jnp
import numpy as np
from jax import lax
from jax.experimental import pallas as pl
from jax.experimental.pallas import tpu as pltpu
from jax.sharding import PartitionSpec as P

SIDE = 192
PARTS = 8
ROWS = SIDE // PARTS
QUADS = ROWS // 4
DUOS = SIDE // 2
CELLS = SIDE * SIDE
COUL = 160.0
PER_CUT = DUOS // 4
PIECES = (PARTS, QUADS, 2 * ROWS, 384)
VECTOR = pl.BlockSpec(memory_space=pltpu.VMEM)
SCALAR = pl.BlockSpec(memory_space=pltpu.SMEM)
F32 = jnp.float32
BF16 = jnp.bfloat16


def cas_matrix():
    index = np.arange(SIDE, dtype=np.int32)
    phases = (index[:, None] * index[None, :] % SIDE).astype(np.float32) * np.float32(2.0 * np.pi / SIDE)
    return np.cos(phases) + np.sin(phases)


CAS = cas_matrix()
BY_PARITY = np.concatenate([np.arange(0, SIDE, 2), np.arange(1, SIDE, 2)])
Y_TABLE = CAS[:, BY_PARITY]
Y_BACK = CAS[BY_PARITY, :]
X_TABLE = CAS[:, BY_PARITY]
X_BACK = CAS[BY_PARITY, :]


def z_tables():
    gap = np.zeros((64, 256), np.float32)
    space = np.zeros((SIDE, 64), np.float32)
    first = np.concatenate([CAS, space], axis=1)
    second = np.concatenate([CAS[:, :128], space, CAS[:, 128:]], axis=1)
    return np.stack([np.concatenate(part, axis=0) for table in (first, second) for part in ((table, gap), (gap, table))])


Z_TABLES = z_tables()
Z_BACKS = np.swapaxes(Z_TABLES, 1, 2)


def wave(index):
    return jnp.where(index < SIDE // 2, index, index - SIDE).astype(F32)


def coulomb(me):
    shape = (ROWS // 2, SIDE, 384)
    pair = lax.broadcasted_iota(jnp.int32, shape, 0)
    row = lax.broadcasted_iota(jnp.int32, shape, 1)
    col = lax.broadcasted_iota(jnp.int32, shape, 2)
    late = jnp.where(col < 256, col >= 128, col >= 320)
    kz = jnp.where(col < 256, col % 128, 128 + col % 64)
    ky = me * ROWS + pair + jnp.where(late, ROWS // 2, 0)
    mx, my, mz = wave(row), wave(ky), wave(kz)
    norm_sq = mx * mx + my * my + mz * mz
    bounded = jnp.maximum(norm_sq, 1.0)
    return jnp.where(norm_sq > 0.5, COUL / bounded, 0.0) / float(SIDE) ** 3


def dot(left, right):
    return jnp.dot(left, right, preferred_element_type=F32)


def tiles(lots, rows):
    return jnp.concatenate([lot[rows, :] for lot in lots], axis=1)


def forward_body(column, target, source, z_tables, y_table, out, *lots):
    def form(duo, carry):
        chunk, part = (duo // PER_CUT) ^ column[0], duo % PER_CUT
        left = target[:, pl.ds(pl.multiple_of(duo * 384, 128), 384)].astype(F32)
        right = source[chunk, :, pl.ds(pl.multiple_of(part * 384, 128), 384)].astype(F32)
        density = left * right
        for tile, lot in enumerate(lots):
            lot[pl.ds(duo, ROWS, stride=DUOS), :] = density[:, tile * 128 : (tile + 1) * 128]
        return carry

    lax.fori_loop(0, DUOS, form, 0, unroll=4)

    def planes(quad, carry):
        along_y = []
        for pair in range(2):
            halves = []
            for plane in range(2):
                rows = pl.ds(pl.multiple_of((quad * 4 + pair * 2 + plane) * DUOS, DUOS), DUOS)
                density = tiles(lots, rows).astype(BF16)
                even = dot(density[:, :256], z_tables[2 * plane])
                odd = dot(density[:, 128:], z_tables[2 * plane + 1])
                halves.append(jnp.concatenate([even, odd], axis=0))
            low, high = halves
            packed = jnp.concatenate([low[:, :128], high[:, :128], low[:, 128:] + high[:, 128:]], axis=1)
            along_y.append(dot(y_table[...], packed.astype(BF16)))
        for part in range(PARTS):
            rows = slice(part * ROWS, (part + 1) * ROWS)
            out[part, quad] = jnp.concatenate([along_y[0][rows], along_y[1][rows]], axis=0).astype(BF16)
        return carry

    lax.fori_loop(0, QUADS, planes, 0)


def forward(column, target, source):
    return pl.pallas_call(
        forward_body,
        in_specs=[SCALAR] + [VECTOR] * 4,
        out_specs=VECTOR,
        out_shape=jax.ShapeDtypeStruct(PIECES, BF16),
        scratch_shapes=[pltpu.VMEM((ROWS * DUOS, 128), F32)] * 3,
        compiler_params=pltpu.CompilerParams(vmem_limit_bytes=32 * 2**20),
        cost_estimate=pl.CostEstimate(flops=1400 * 10**6, bytes_accessed=7 * 10**6, transcendentals=0),
        name="forward_zy",
    )(column, target, source, jnp.asarray(Z_TABLES, BF16), jnp.asarray(Y_TABLE, BF16))


def middle_body(pieces, kernel, x_table, x_back, out, head0, head1, tail):
    lots = (head0, head1, tail)
    block = QUADS * 2 * ROWS
    for part in range(PARTS):
        for tile, lot in enumerate(lots):
            lot[part * block : (part + 1) * block] = (
                pieces[part, :, :, tile * 128 : (tile + 1) * 128].astype(F32).reshape(block, 128)
            )
    low = lax.broadcasted_iota(jnp.int32, (DUOS, 128), 1) < 64

    def step(i, carry):
        here = pl.ds(i, DUOS, stride=ROWS)
        there = pl.ds(i + ROWS // 2, DUOS, stride=ROWS)
        tail_a, tail_b = tail[here, :], tail[there, :]
        tail_first = jnp.where(low, tail_a, pltpu.roll(tail_b, 64, 1))
        tail_second = jnp.where(low, pltpu.roll(tail_a, 64, 1), tail_b)
        columns = jnp.concatenate(
            [
                jnp.concatenate([head0[here, :], head0[there, :], tail_first], axis=1),
                jnp.concatenate([head1[here, :], head1[there, :], tail_second], axis=1),
            ],
            axis=0,
        ).astype(BF16)
        spectrum = (kernel[i] * dot(x_table[...], columns)).astype(BF16)
        back = dot(x_back[...], spectrum)
        head0[here, :] = back[:DUOS, :128]
        head1[here, :] = back[DUOS:, :128]
        head0[there, :] = back[:DUOS, 128:256]
        head1[there, :] = back[DUOS:, 128:256]
        first, second = back[:DUOS, 256:], back[DUOS:, 256:]
        tail[here, :] = jnp.where(low, first, pltpu.roll(second, 64, 1))
        tail[there, :] = jnp.where(low, pltpu.roll(first, 64, 1), second)
        return carry

    lax.fori_loop(0, ROWS // 2, step, 0)
    for part in range(PARTS):
        for tile, lot in enumerate(lots):
            out[part, :, :, tile * 128 : (tile + 1) * 128] = (
                lot[part * block : (part + 1) * block].astype(BF16).reshape(QUADS, 2 * ROWS, 128)
            )


def middle(pieces, kernel):
    return pl.pallas_call(
        middle_body,
        in_specs=[VECTOR] * 4,
        out_specs=VECTOR,
        out_shape=jax.ShapeDtypeStruct(PIECES, BF16),
        scratch_shapes=[pltpu.VMEM((DUOS * ROWS, 128), F32)] * 3,
        compiler_params=pltpu.CompilerParams(vmem_limit_bytes=32 * 2**20),
        cost_estimate=pl.CostEstimate(flops=1400 * 10**6, bytes_accessed=7 * 10**6, transcendentals=0),
        name="middle_x",
    )(pieces, kernel, jnp.asarray(X_TABLE, BF16), jnp.asarray(X_BACK, BF16))


def backward_body(column, pieces, source, *refs):
    (total, y_table, z_tables, out), lots = ((None,) + refs[:3], refs[3:]) if len(refs) == 6 else (refs[:4], refs[4:])

    def planes(quad, carry):
        parts = [pieces[part, quad].astype(F32) for part in range(PARTS)]
        for pair in range(2):
            stack = jnp.concatenate([part[pair * ROWS : (pair + 1) * ROWS] for part in parts], axis=0)
            fields = dot(y_table[...], stack.astype(BF16)).astype(BF16)
            for plane in range(2):
                lanes = fields[:, 128:] if plane else jnp.concatenate([fields[:, :128], fields[:, 256:]], axis=1)
                even = dot(lanes[:DUOS], z_tables[2 * plane])
                odd = dot(lanes[DUOS:], z_tables[2 * plane + 1])
                rows = pl.ds(pl.multiple_of((quad * 4 + pair * 2 + plane) * DUOS, DUOS), DUOS)
                lots[0][rows, :] = even[:, :128]
                lots[1][rows, :] = even[:, 128:] + odd[:, :128]
                lots[2][rows, :] = odd[:, 128:]
        return carry

    lax.fori_loop(0, QUADS, planes, 0)

    def gather(duo, carry):
        chunk, part = (duo // PER_CUT) ^ column[0], duo % PER_CUT
        potential = tiles(lots, pl.ds(duo, ROWS, stride=DUOS))
        here = pl.ds(pl.multiple_of(duo * 384, 128), 384)
        right = source[chunk, :, pl.ds(pl.multiple_of(part * 384, 128), 384)].astype(F32)
        term = potential * right
        out[:, here] = -term if total is None else total[:, here] - term
        return carry

    lax.fori_loop(0, DUOS, gather, 0, unroll=4)


def backward(column, pieces, source, total):
    return pl.pallas_call(
        backward_body,
        in_specs=[SCALAR] + [VECTOR] * (4 + (total is not None)),
        out_specs=VECTOR,
        out_shape=jax.ShapeDtypeStruct((ROWS, CELLS), F32),
        scratch_shapes=[pltpu.VMEM((ROWS * DUOS, 128), F32)] * 3,
        compiler_params=pltpu.CompilerParams(vmem_limit_bytes=32 * 2**20),
        cost_estimate=pl.CostEstimate(flops=1400 * 10**6, bytes_accessed=7 * 10**6, transcendentals=0),
        name="backward_yz",
    )(column, pieces, source, *([] if total is None else [total]), jnp.asarray(Y_BACK, BF16), jnp.asarray(Z_BACKS, BF16))


BOTH = ("band", "grid")
CHIPS = [(x, y, z) for x in range(4) for y in range(4) for z in range(8)]


def place(x, y, z, core):
    return ((z % 8 // 2) * 8 + x * 2 + core) * PARTS + y * 2 + z % 2


def exchange_groups():
    groups = [[place(x, y, 2 * k + low, 0) for y in range(4) for low in range(2)] for x in range(4) for k in range(4)]
    for y in range(4):
        for k in range(4):
            groups.append([place(slab ^ y, y, 2 * k + 2 - low, 1) for slab in range(4) for low in range(2)])
    return groups


def exchange(pieces):
    return lax.all_to_all(pieces, BOTH, 0, 0, axis_index_groups=exchange_groups(), tiled=True)


def turned(x, y, z, which):
    step = (2 if z % 2 == 0 else 0) if which == 0 else (-2 if z % 2 else 0)
    return x ^ y, x, (z + step) % 8


def move(array, pairs):
    return lax.ppermute(array, BOTH, pairs)


def spread(orbital, is_root):
    cut = CELLS // 4
    cuts = [orbital[:, step * cut : (step + 1) * cut] for step in range(4)]
    slabs = [(y, low) for y in range(4) for low in range(2)]
    mine = sum(
        move(cuts[step], [(place(0, y, z + low, 0), place(step, y, z + low, z // 4)) for z in (0, 4) for y, low in slabs])
        for step in range(4)
    )
    away = sum(
        move(
            mine,
            [(place(x, y, 4 * c + low, c), place(x, y, 4 * c + low + up, c)) for c in range(2) for x in range(4) for y, low in slabs],
        )
        for up in (2, 6, 4)
    )
    mine = jnp.where(is_root, mine, away)
    got = []
    for step in range(4):
        pairs = [(place(x, y, z, 0), place(x ^ step, y, z, 0)) for x, y, z in CHIPS]
        pairs += [(place(x, y, z, 1), place(x ^ step, y ^ x ^ step, z, 1)) for x, y, z in CHIPS]
        got.append(move(mine, pairs))
    return jnp.stack(got)


def local(orbitals):
    band, grid = lax.axis_index("band"), lax.axis_index("grid")
    z_hi, x, core = band // 8, (band // 2) % 4, band % 2
    y, low = grid // 2, grid % 2
    column = x[None].astype(jnp.int32)
    kernel = coulomb(2 * jnp.where(core == 0, y, x ^ y) + low)
    own = orbitals[0]

    sources = [spread(orbitals[p], z_hi == 2 * core) for p in range(2)]
    out_a = [(place(x, y, z, 0), place(*turned(x, y, z, 0), 1)) for x, y, z in CHIPS]
    out_b = [(place(x, y, z, 1), place(*turned(x, y, z, 1), 1)) for x, y, z in CHIPS]
    target_a = jnp.where(core == 0, own, move(own, out_a))
    swap = [(place(x, y, z, 1), place(x, y, z, 0)) for x, y, z in CHIPS]
    target_b = move(own, swap) + move(own, out_b)
    targets = [target_a, target_b]

    there = {}
    for p in range(2):
        for t in range(2):
            there[p, t] = exchange(forward(column, targets[t], sources[p]))
    sums = []
    for t in range(2):
        total = None
        for p in range(2):
            total = backward(column, exchange(middle(there[p, t], kernel)), sources[p], total)
        sums.append(total)
    sum_a, sum_b = sums
    back_a = move(sum_a.astype(BF16), [(b, a) for a, b in out_a])
    back_b = move(sum_b.astype(BF16), [(b, a) for a, b in out_b])
    swapped = move(sum_b, [(b, a) for a, b in swap])
    result = jnp.where(core == 0, sum_a, swapped) + jnp.where(core == 0, back_a, back_b).astype(F32)
    return result[None]


def solution(mesh):
    return jax.shard_map(
        local,
        mesh=mesh,
        in_specs=(P("band", "grid", None),),
        out_specs=P("band", "grid", None),
        check_vma=False,
    )
```

time: 332 us -> 446 us (1.34)
  the two profiles are of different devices: /device:TPU:32 before, /device:TPU:100 now
where the time goes in v3:
time: 446 us; the launch traced here: 444 us
  waiting for transfers between devices  164 us (37%)
  starting transfers between devices  133 us (30%)
  Pallas kernels  101 us (23%)
  local copies, waits for them, and re-layouts  32.5 us (7%)
  other arithmetic  13.3 us (3%)
    ppermute x28, waiting for transfers between devices, move(): return lax.ppermute(array, BOTH, pairs)  147 us
    ppermute x28, starting transfers between devices, move(): return lax.ppermute(array, BOTH, pairs)  68.9 us
    all_to_all x8, starting transfers between devices, exchange(): lax.all_to_all(pieces, BOTH, 0, 0, axis_index_groups=exchange_groups(), t...  63.7 us
    pallas_call x4, Pallas kernels, backward(): pl.pallas_call(backward_body, in_specs=[SCALAR] + [VECTOR] * (4 + (total...  35.2 us
    pallas_call x4, Pallas kernels, forward(): pl.pallas_call(forward_body, in_specs=[SCALAR] + [VECTOR] * 4, out_specs=...  33.1 us
    pallas_call x4, Pallas kernels, middle(): pl.pallas_call(middle_body, in_specs=[VECTOR] * 4, out_specs=VECTOR, out_...  32.7 us
    unnamed x82, local copies, waits for them, and re-layouts  29.1 us
    all_to_all x8, waiting for transfers between devices, exchange(): lax.all_to_all(pieces, BOTH, 0, 0, axis_index_groups=exchange_groups(), t...  16.3 us
  transfers between devices with their start and end apart: 36, of which 11 were waited for; matrix products, arithmetic and copies ran while one was open for 3% of the time, Pallas kernels for 23%

profile of v3, /device:TPU:100, one launch (start us, length us, event | category | flops | bytes accessed | tf_op | source)
XLA Modules:
  0.0 443.6 jit_solution(9021303945999608759)
XLA Ops:
  5.2 5.8 %collective-permute-start = (bf16[24,36864]{1,0:T(8,128)(2,1)S(1)}, bf16[24,36864]{1,0:T(8,128)(2,1)}, u32[]{:S(2)}, u32[]{:S(2)}) collective-permute-start(bf16[24,36864]{1,0:T(8,128)(2,1)S(1)} %get-tuple-element.6), channel_id=1, source_target_pairs={{0,72},{1,9},{64,136},{65,73},{128,200},{129,137},{192,8},{193,201... | collective-permute-start | bytes 5308424 | tf_op jit(solution)/shard_map/ppermute | solution.py:248
  17.7 28.8 %collective-permute-done.5 = bf16[24,9216]{1,0:T(8,128)(2,1)} collective-permute-done((bf16[24,9216]{1,0:T(8,128)(2,1)S(1)}, bf16[24,9216]{1,0:T(8,128)(2,1)}, u32[]{:S(2)}, u32[]{:S(2)}) %collective-permute-start.5) | collective-permute-done | bytes 442400 | tf_op jit(solution)/shard_map/ppermute | solution.py:248
  56.3 6.1 %collective-permute-done.11 = bf16[24,9216]{1,0:T(8,128)(2,1)S(1)} collective-permute-done((bf16[24,9216]{1,0:T(8,128)(2,1)S(1)}, bf16[24,9216]{1,0:T(8,128)(2,1)S(1)}, u32[]{:S(2)}, u32[]{:S(2)}) %collective-permute-start.11) | collective-permute-done | bytes 442400 | tf_op jit(solution)/shard_map/ppermute | solution.py:248
  68.4 9.2 %forward_zy.4 = bf16[8,6,48,384]{3,2,1,0:T(8,128)(2,1)} custom-call(s32[1]{0:T(128)} %bitcast.column, bf16[24,36864]{1,0:T(8,128)(2,1)S(1)} %broadcast_select_fusion.target, bf16[4,24,9216]{2,1,0:T(8,128)(2,1)S(1)} %pad_maximum_fusion.source, bf16[4,256,256]{2,1,0:T(8,128)(2,1)S(1)} %copy-done.10, bf16[192,192]{1,0:T(8,128)(2,1)S(1)} %copy-done.30), custom_call_target="tpu_custom_call" | custom-call | flops 1400000000 | bytes 7000000 | tf_op jit(solution)/shard_map/forward_zy/pallas_call | solution.py:110
  78.8 16.9 %all-to-all-start = ((bf16[8,6,48,384]{3,2,1,0:T(8,128)(2,1)}), bf16[8,6,48,384]{3,2,1,0:T(8,128)(2,1)}, u32[]{:S(2)}, u32[]{:S(2)}) async-start(bf16[8,6,48,384]{3,2,1,0:T(8,128)(2,1)} %forward_zy.4), calls=%async_computation | async-start | bytes 3538944 | tf_op jit(solution)/shard_map/all_to_all | solution.py:239
  104.5 18.2 %collective-permute-done.22 = bf16[24,9216]{1,0:T(8,128)(2,1)S(1)} collective-permute-done((bf16[24,9216]{1,0:T(8,128)(2,1)S(1)}, bf16[24,9216]{1,0:T(8,128)(2,1)S(1)}, u32[]{:S(2)}, u32[]{:S(2)}) %collective-permute-start.22) | collective-permute-done | bytes 442400 | tf_op jit(solution)/shard_map/ppermute | solution.py:248
  126.6 8.0 %forward_zy.5 = bf16[8,6,48,384]{3,2,1,0:T(8,128)(2,1)S(1)} custom-call(s32[1]{0:T(128)} %bitcast.column, bf16[24,36864]{1,0:T(8,128)(2,1)S(1)} %copy-done.5, bf16[4,24,9216]{2,1,0:T(8,128)(2,1)S(1)} %pad_maximum_fusion.1.source, bf16[4,256,256]{2,1,0:T(8,128)(2,1)S(1)} %copy-done.11, bf16[192,192]{1,0:T(8,128)(2,1)S(1)} %copy-done.31), custom_call_target="tpu_custom_call" | custom-call | flops 1400000000 | bytes 7000000 | tf_op jit(solution)/shard_map/forward_zy/pallas_call | solution.py:110
  135.8 9.7 %all-to-all-start.2 = ((bf16[8,6,48,384]{3,2,1,0:T(8,128)(2,1)}), bf16[8,6,48,384]{3,2,1,0:T(8,128)(2,1)}, u32[]{:S(2)}, u32[]{:S(2)}) async-start(bf16[8,6,48,384]{3,2,1,0:T(8,128)(2,1)} %copy-done.21), calls=%async_computation.2 | async-start | bytes 3538944 | tf_op jit(solution)/shard_map/all_to_all | solution.py:239
  147.7 11.6 %collective-permute-done.23 = bf16[24,36864]{1,0:T(8,128)(2,1)S(1)} collective-permute-done((bf16[24,36864]{1,0:T(8,128)(2,1)}, bf16[24,36864]{1,0:T(8,128)(2,1)S(1)}, u32[]{:S(2)}, u32[]{:S(2)}) %collective-permute-start.23) | collective-permute-done | bytes 1769504 | tf_op jit(solution)/shard_map/ppermute | solution.py:248
  159.7 8.0 %forward_zy.6 = bf16[8,6,48,384]{3,2,1,0:T(8,128)(2,1)S(1)} custom-call(s32[1]{0:T(128)} %bitcast.column, bf16[24,36864]{1,0:T(8,128)(2,1)S(1)} %add.109.target, bf16[4,24,9216]{2,1,0:T(8,128)(2,1)S(1)} %pad_maximum_fusion.source, bf16[4,256,256]{2,1,0:T(8,128)(2,1)S(1)} %copy-done.12, bf16[192,192]{1,0:T(8,128)(2,1)S(1)} %copy-done.32), custom_call_target="tpu_custom_call" | custom-call | flops 1400000000 | bytes 7000000 | tf_op jit(solution)/shard_map/forward_zy/pallas_call | solution.py:110
  170.2 11.0 %all-to-all-start.4 = ((bf16[8,6,48,384]{3,2,1,0:T(8,128)(2,1)}), bf16[8,6,48,384]{3,2,1,0:T(8,128)(2,1)}, u32[]{:S(2)}, u32[]{:S(2)}) async-start(bf16[8,6,48,384]{3,2,1,0:T(8,128)(2,1)} %copy-done.22), calls=%async_computation.4 | async-start | bytes 3538944 | tf_op jit(solution)/shard_map/all_to_all | solution.py:239
  183.2 8.0 %forward_zy.7 = bf16[8,6,48,384]{3,2,1,0:T(8,128)(2,1)S(1)} custom-call(s32[1]{0:T(128)} %bitcast.column, bf16[24,36864]{1,0:T(8,128)(2,1)S(1)} %copy-done.7, bf16[4,24,9216]{2,1,0:T(8,128)(2,1)S(1)} %pad_maximum_fusion.1.source, bf16[4,256,256]{2,1,0:T(8,128)(2,1)S(1)} %copy-done.13, bf16[192,192]{1,0:T(8,128)(2,1)S(1)} %copy-done.33), custom_call_target="tpu_custom_call" | custom-call | flops 1400000000 | bytes 7000000 | tf_op jit(solution)/shard_map/forward_zy/pallas_call | solution.py:110
  192.5 6.0 %all-to-all-done.4.pieces = bf16[8,6,48,384]{3,2,1,0:T(8,128)(2,1)} async-done(((bf16[8,6,48,384]{3,2,1,0:T(8,128)(2,1)}), bf16[8,6,48,384]{3,2,1,0:T(8,128)(2,1)}, u32[]{:S(2)}, u32[]{:S(2)}) %all-to-all-start.4) | async-done | bytes 1769504 | tf_op jit(solution)/shard_map/all_to_all | solution.py:239
  205.9 8.2 %middle_x.5 = bf16[8,6,48,384]{3,2,1,0:T(8,128)(2,1)S(1)} custom-call(bf16[8,6,48,384]{3,2,1,0:T(8,128)(2,1)} %all-to-all-done.2.pieces, f32[12,192,384]{2,1,0:T(8,128)S(1)} %select_multiply_fusion.kernel, bf16[192,192]{1,0:T(8,128)(2,1)S(1)} %copy-done.34, bf16[192,192]{1,0:T(8,128)(2,1)S(1)} %copy-done.23), custom_call_target="tpu_custom_call" | custom-call | flops 1400000000 | bytes 7000000 | tf_op jit(solution)/shard_map/middle_x/pallas_call | solution.py:165
  216.1 5.4 %all-to-all-start.3 = ((bf16[8,6,48,384]{3,2,1,0:T(8,128)(2,1)}), bf16[8,6,48,384]{3,2,1,0:T(8,128)(2,1)}, u32[]{:S(2)}, u32[]{:S(2)}) async-start(bf16[8,6,48,384]{3,2,1,0:T(8,128)(2,1)} %copy-done.18), calls=%async_computation.3 | async-start | bytes 3538944 | tf_op jit(solution)/shard_map/all_to_all | solution.py:239
  223.3 8.2 %middle_x.6 = bf16[8,6,48,384]{3,2,1,0:T(8,128)(2,1)S(1)} custom-call(bf16[8,6,48,384]{3,2,1,0:T(8,128)(2,1)} %all-to-all-done.4.pieces, f32[12,192,384]{2,1,0:T(8,128)S(1)} %select_multiply_fusion.kernel, bf16[192,192]{1,0:T(8,128)(2,1)S(1)} %copy-done.35, bf16[192,192]{1,0:T(8,128)(2,1)S(1)} %copy-done.24), custom_call_target="tpu_custom_call" | custom-call | flops 1400000000 | bytes 7000000 | tf_op jit(solution)/shard_map/middle_x/pallas_call | solution.py:165
  243.1 8.2 %middle_x.7 = bf16[8,6,48,384]{3,2,1,0:T(8,128)(2,1)S(1)} custom-call(bf16[8,6,48,384]{3,2,1,0:T(8,128)(2,1)} %all-to-all-done.6.pieces, f32[12,192,384]{2,1,0:T(8,128)S(1)} %select_multiply_fusion.kernel, bf16[192,192]{1,0:T(8,128)(2,1)S(1)} %copy-done.36, bf16[192,192]{1,0:T(8,128)(2,1)S(1)} %copy-done.25), custom_call_target="tpu_custom_call" | custom-call | flops 1400000000 | bytes 7000000 | tf_op jit(solution)/shard_map/middle_x/pallas_call | solution.py:165
  262.8 8.2 %middle_x.4 = bf16[8,6,48,384]{3,2,1,0:T(8,128)(2,1)S(1)} custom-call(bf16[8,6,48,384]{3,2,1,0:T(8,128)(2,1)} %all-to-all-done.pieces, f32[12,192,384]{2,1,0:T(8,128)S(1)} %select_multiply_fusion.kernel, bf16[192,192]{1,0:T(8,128)(2,1)S(1)} %copy-done.37, bf16[192,192]{1,0:T(8,128)(2,1)S(1)} %copy-done.26), custom_call_target="tpu_custom_call" | custom-call | flops 1400000000 | bytes 7000000 | tf_op jit(solution)/shard_map/middle_x/pallas_call | solution.py:165
  282.7 7.9 %backward_yz.6.refs_0_ = f32[24,36864]{1,0:T(8,128)S(1)} custom-call(s32[1]{0:T(128)} %bitcast.column, bf16[8,6,48,384]{3,2,1,0:T(8,128)(2,1)} %all-to-all-done.7.pieces, bf16[4,24,9216]{2,1,0:T(8,128)(2,1)S(1)} %copy-done.1, bf16[192,192]{1,0:T(8,128)(2,1)S(1)} %copy-done.27, bf16[4,256,256]{2,1,0:T(8,128)(2,1)S(1)} %copy-done.14), custom_call_target="tpu_custom_call" | custom-call | flops 1400000000 | bytes 7000000 | tf_op jit(solution)/shard_map/backward_yz/pallas_call | solution.py:210
  290.6 10.7 %backward_yz.7 = f32[24,36864]{1,0:T(8,128)} custom-call(s32[1]{0:T(128)} %bitcast.column, bf16[8,6,48,384]{3,2,1,0:T(8,128)(2,1)} %all-to-all-done.5.pieces, bf16[4,24,9216]{2,1,0:T(8,128)(2,1)S(1)} %copy-done.3, f32[24,36864]{1,0:T(8,128)S(1)} %backward_yz.6.refs_0_, bf16[192,192]{1,0:T(8,128)(2,1)S(1)} %copy-done.28, bf16[4,256,256]{2,1,0:T(8,128)(2,1)S(1)} %copy-done.14), custom_call_target="tpu_custom_call" | custom-call | flops 1400000000 | bytes 7000000 | tf_op jit(solution)/shard_map/backward_yz/pallas_call | solution.py:210
  301.3 32.6 %collective-permute-start.25 = (f32[24,36864]{1,0:T(8,128)}, f32[24,36864]{1,0:T(8,128)}, u32[]{:S(2)}, u32[]{:S(2)}) collective-permute-start(f32[24,36864]{1,0:T(8,128)} %backward_yz.7), channel_id=1, source_target_pairs={{0,8},{1,9},{64,72},{65,73},{128,136},{129,137},{192,200},{193,201... | collective-permute-start | bytes 10616840 | tf_op jit(solution)/shard_map/ppermute | solution.py:248
  337.4 7.7 %backward_yz.4.refs_0_ = f32[24,36864]{1,0:T(8,128)S(1)} custom-call(s32[1]{0:T(128)} %bitcast.column, bf16[8,6,48,384]{3,2,1,0:T(8,128)(2,1)} %all-to-all-done.3.pieces, bf16[4,24,9216]{2,1,0:T(8,128)(2,1)S(1)} %copy-done.1, bf16[192,192]{1,0:T(8,128)(2,1)S(1)} %copy-done.28, bf16[4,256,256]{2,1,0:T(8,128)(2,1)S(1)} %copy-done.14), custom_call_target="tpu_custom_call" | custom-call | flops 1400000000 | bytes 7000000 | tf_op jit(solution)/shard_map/backward_yz/pallas_call | solution.py:210
  350.9 8.9 %backward_yz.5 = f32[24,36864]{1,0:T(8,128)S(1)} custom-call(s32[1]{0:T(128)} %bitcast.column, bf16[8,6,48,384]{3,2,1,0:T(8,128)(2,1)} %all-to-all-done.1.pieces, bf16[4,24,9216]{2,1,0:T(8,128)(2,1)S(1)} %copy-done.3, f32[24,36864]{1,0:T(8,128)S(1)} %copy-done.9, bf16[192,192]{1,0:T(8,128)(2,1)S(1)} %copy-done.29, bf16[4,256,256]{2,1,0:T(8,128)(2,1)S(1)} %copy-done.15), custom_call_target="tpu_custom_call" | custom-call | flops 1400000000 | bytes 7000000 | tf_op jit(solution)/shard_map/backward_yz/pallas_call | solution.py:210
  362.2 78.9 %collective-permute-done.26 = bf16[24,36864]{1,0:T(8,128)(2,1)S(1)} collective-permute-done((bf16[24,36864]{1,0:T(8,128)(2,1)S(1)}, bf16[24,36864]{1,0:T(8,128)(2,1)S(1)}, u32[]{:S(2)}, u32[]{:S(2)}) %collective-permute-start.26) | collective-permute-done | bytes 1769504 | tf_op jit(solution)/shard_map/ppermute | solution.py:248
  (165 shorter events, 110.9 us)
Async XLA Ops:
  5.2 61.7 %collective-permute-start = (bf16[24,36864]{1,0:T(8,128)(2,1)S(1)}, bf16[24,36864]{1,0:T(8,128)(2,1)}, u32[]{:S(2)}, u32[]{:S(2)}) collective-permute-start(bf16[24,36864]{1,0:T(8,128)(2,1)S(1)} %get-tuple-element.6), channel_id=1, source_target_pairs={{0,72},{1,9},{64,136},{65,73},{128,200},{129,137},{192,8},{193,201... | collective-permute-start | bytes 5308424 | tf_op jit(solution)/shard_map/ppermute | solution.py:248
  11.8 34.7 %collective-permute-start.5 = (bf16[24,9216]{1,0:T(8,128)(2,1)S(1)}, bf16[24,9216]{1,0:T(8,128)(2,1)}, u32[]{:S(2)}, u32[]{:S(2)}) collective-permute-start(bf16[24,9216]{1,0:T(8,128)(2,1)S(1)} %add_add_fusion.1), channel_id=1, source_target_pairs={{0,64},{1,65},{2,66},{3,67},{4,68},{5,69},{6,70},{7,71},{16,80},{1... | collective-permute-start | bytes 1327112 | tf_op jit(solution)/shard_map/ppermute | solution.py:248
  13.1 34.1 %collective-permute-start.6 = (bf16[24,9216]{1,0:T(8,128)(2,1)S(1)}, bf16[24,9216]{1,0:T(8,128)(2,1)}, u32[]{:S(2)}, u32[]{:S(2)}) collective-permute-start(bf16[24,9216]{1,0:T(8,128)(2,1)S(1)} %add_add_fusion.1), channel_id=1, source_target_pairs={{0,192},{1,193},{2,194},{3,195},{4,196},{5,197},{6,198},{7,199},{1... | collective-permute-start | bytes 1327112 | tf_op jit(solution)/shard_map/ppermute | solution.py:248
  15.6 33.9 %collective-permute-start.15 = (bf16[24,9216]{1,0:T(8,128)(2,1)}, bf16[24,9216]{1,0:T(8,128)(2,1)}, u32[]{:S(2)}, u32[]{:S(2)}) collective-permute-start(bf16[24,9216]{1,0:T(8,128)(2,1)} %get-tuple-element.8), channel_id=1, source_target_pairs={{0,48},{1,49},{2,50},{3,51},{4,52},{5,53},{6,54},{7,55},{128,184},... | collective-permute-start | bytes 1327112 | tf_op jit(solution)/shard_map/ppermute | solution.py:248
  17.0 32.6 %collective-permute-start.14 = (bf16[24,9216]{1,0:T(8,128)(2,1)}, bf16[24,9216]{1,0:T(8,128)(2,1)S(1)}, u32[]{:S(2)}, u32[]{:S(2)}) collective-permute-start(bf16[24,9216]{1,0:T(8,128)(2,1)} %get-tuple-element.9), channel_id=1, source_target_pairs={{0,32},{1,33},{2,34},{3,35},{4,36},{5,37},{6,38},{7,39},{128,168},... | collective-permute-start | bytes 1327112 | tf_op jit(solution)/shard_map/ppermute | solution.py:248
  49.6 14.3 %collective-permute-start.10 = (bf16[24,9216]{1,0:T(8,128)(2,1)S(1)}, bf16[24,9216]{1,0:T(8,128)(2,1)S(1)}, u32[]{:S(2)}, u32[]{:S(2)}) collective-permute-start(bf16[24,9216]{1,0:T(8,128)(2,1)S(1)} %add_select_fusion.1), channel_id=1, source_target_pairs={{0,32},{1,33},{64,96},{65,97},{128,160},{129,161},{192,224},{193,2... | collective-permute-start | bytes 1327112 | tf_op jit(solution)/shard_map/ppermute | solution.py:248
  62.4 33.3 %collective-permute-start.18 = (bf16[24,9216]{1,0:T(8,128)(2,1)}, bf16[24,9216]{1,0:T(8,128)(2,1)}, u32[]{:S(2)}, u32[]{:S(2)}) collective-permute-start(bf16[24,9216]{1,0:T(8,128)(2,1)} %add_add_fusion), channel_id=1, source_target_pairs={{0,128},{1,129},{2,130},{3,131},{4,132},{5,133},{6,134},{7,135},{1... | collective-permute-start | bytes 1327112 | tf_op jit(solution)/shard_map/ppermute | solution.py:248
  63.9 31.8 %collective-permute-start.16 = (bf16[24,9216]{1,0:T(8,128)(2,1)}, bf16[24,9216]{1,0:T(8,128)(2,1)}, u32[]{:S(2)}, u32[]{:S(2)}) collective-permute-start(bf16[24,9216]{1,0:T(8,128)(2,1)} %add_add_fusion), channel_id=1, source_target_pairs={{0,64},{1,65},{2,66},{3,67},{4,68},{5,69},{6,70},{7,71},{16,80},{1... | collective-permute-start | bytes 1327112 | tf_op jit(solution)/shard_map/ppermute | solution.py:248
  65.2 30.5 %collective-permute-start.17 = (bf16[24,9216]{1,0:T(8,128)(2,1)}, bf16[24,9216]{1,0:T(8,128)(2,1)}, u32[]{:S(2)}, u32[]{:S(2)}) collective-permute-start(bf16[24,9216]{1,0:T(8,128)(2,1)} %add_add_fusion), channel_id=1, source_target_pairs={{0,192},{1,193},{2,194},{3,195},{4,196},{5,197},{6,198},{7,199},{1... | collective-permute-start | bytes 1327112 | tf_op jit(solution)/shard_map/ppermute | solution.py:248
  78.8 57.0 %all-to-all-start = ((bf16[8,6,48,384]{3,2,1,0:T(8,128)(2,1)}), bf16[8,6,48,384]{3,2,1,0:T(8,128)(2,1)}, u32[]{:S(2)}, u32[]{:S(2)}) async-start(bf16[8,6,48,384]{3,2,1,0:T(8,128)(2,1)} %forward_zy.4), calls=%async_computation | async-start | bytes 3538944 | tf_op jit(solution)/shard_map/all_to_all | solution.py:239
  97.2 25.5 %collective-permute-start.22 = (bf16[24,9216]{1,0:T(8,128)(2,1)S(1)}, bf16[24,9216]{1,0:T(8,128)(2,1)S(1)}, u32[]{:S(2)}, u32[]{:S(2)}) collective-permute-start(bf16[24,9216]{1,0:T(8,128)(2,1)S(1)} %add_select_fusion), channel_id=1, source_target_pairs={{0,48},{1,49},{64,112},{65,113},{128,176},{129,177},{192,240},{193... | collective-permute-start | bytes 1327112 | tf_op jit(solution)/shard_map/ppermute | solution.py:248
  101.7 21.1 %collective-permute-start.21 = (bf16[24,9216]{1,0:T(8,128)(2,1)S(1)}, bf16[24,9216]{1,0:T(8,128)(2,1)S(1)}, u32[]{:S(2)}, u32[]{:S(2)}) collective-permute-start(bf16[24,9216]{1,0:T(8,128)(2,1)S(1)} %add_select_fusion), channel_id=1, source_target_pairs={{0,32},{1,33},{64,96},{65,97},{128,160},{129,161},{192,224},{193,2... | collective-permute-start | bytes 1327112 | tf_op jit(solution)/shard_map/ppermute | solution.py:248
  101.7 24.7 %collective-permute-start.20 = (bf16[24,9216]{1,0:T(8,128)(2,1)S(1)}, bf16[24,9216]{1,0:T(8,128)(2,1)S(1)}, u32[]{:S(2)}, u32[]{:S(2)}) collective-permute-start(bf16[24,9216]{1,0:T(8,128)(2,1)S(1)} %add_select_fusion), channel_id=1, source_target_pairs={{0,16},{1,17},{64,80},{65,81},{128,144},{129,145},{192,208},{193,2... | collective-permute-start | bytes 1327112 | tf_op jit(solution)/shard_map/ppermute | solution.py:248
  103.8 22.5 %collective-permute-start.19 = (bf16[24,9216]{1,0:T(8,128)(2,1)S(1)}, bf16[24,9216]{1,0:T(8,128)(2,1)S(1)}, u32[]{:S(2)}, u32[]{:S(2)}) collective-permute-start(bf16[24,9216]{1,0:T(8,128)(2,1)S(1)} %add_select_fusion), channel_id=1, source_target_pairs={{0,0},{1,1},{64,64},{65,65},{128,128},{129,129},{192,192},{193,193... | collective-permute-start | bytes 1327112 | tf_op jit(solution)/shard_map/ppermute | solution.py:248
  135.8 34.4 %all-to-all-start.2 = ((bf16[8,6,48,384]{3,2,1,0:T(8,128)(2,1)}), bf16[8,6,48,384]{3,2,1,0:T(8,128)(2,1)}, u32[]{:S(2)}, u32[]{:S(2)}) async-start(bf16[8,6,48,384]{3,2,1,0:T(8,128)(2,1)} %copy-done.21), calls=%async_computation.2 | async-start | bytes 3538944 | tf_op jit(solution)/shard_map/all_to_all | solution.py:239
  170.2 28.3 %all-to-all-start.4 = ((bf16[8,6,48,384]{3,2,1,0:T(8,128)(2,1)}), bf16[8,6,48,384]{3,2,1,0:T(8,128)(2,1)}, u32[]{:S(2)}, u32[]{:S(2)}) async-start(bf16[8,6,48,384]{3,2,1,0:T(8,128)(2,1)} %copy-done.22), calls=%async_computation.4 | async-start | bytes 3538944 | tf_op jit(solution)/shard_map/all_to_all | solution.py:239
  198.5 17.6 %all-to-all-start.6 = ((bf16[8,6,48,384]{3,2,1,0:T(8,128)(2,1)}), bf16[8,6,48,384]{3,2,1,0:T(8,128)(2,1)}, u32[]{:S(2)}, u32[]{:S(2)}) async-start(bf16[8,6,48,384]{3,2,1,0:T(8,128)(2,1)} %copy-done.20), calls=%async_computation.6 | async-start | bytes 3538944 | tf_op jit(solution)/shard_map/all_to_all | solution.py:239
  216.1 19.8 %all-to-all-start.3 = ((bf16[8,6,48,384]{3,2,1,0:T(8,128)(2,1)}), bf16[8,6,48,384]{3,2,1,0:T(8,128)(2,1)}, u32[]{:S(2)}, u32[]{:S(2)}) async-start(bf16[8,6,48,384]{3,2,1,0:T(8,128)(2,1)} %copy-done.18), calls=%async_computation.3 | async-start | bytes 3538944 | tf_op jit(solution)/shard_map/all_to_all | solution.py:239
  235.9 19.7 %all-to-all-start.5 = ((bf16[8,6,48,384]{3,2,1,0:T(8,128)(2,1)}), bf16[8,6,48,384]{3,2,1,0:T(8,128)(2,1)}, u32[]{:S(2)}, u32[]{:S(2)}) async-start(bf16[8,6,48,384]{3,2,1,0:T(8,128)(2,1)} %copy-done.19), calls=%async_computation.5 | async-start | bytes 3538944 | tf_op jit(solution)/shard_map/all_to_all | solution.py:239
  255.6 19.7 %all-to-all-start.7 = ((bf16[8,6,48,384]{3,2,1,0:T(8,128)(2,1)}), bf16[8,6,48,384]{3,2,1,0:T(8,128)(2,1)}, u32[]{:S(2)}, u32[]{:S(2)}) async-start(bf16[8,6,48,384]{3,2,1,0:T(8,128)(2,1)} %copy-done.17), calls=%async_computation.7 | async-start | bytes 3538944 | tf_op jit(solution)/shard_map/all_to_all | solution.py:239
  275.4 71.6 %all-to-all-start.1 = ((bf16[8,6,48,384]{3,2,1,0:T(8,128)(2,1)}), bf16[8,6,48,384]{3,2,1,0:T(8,128)(2,1)}, u32[]{:S(2)}, u32[]{:S(2)}) async-start(bf16[8,6,48,384]{3,2,1,0:T(8,128)(2,1)} %copy-done.16), calls=%async_computation.1 | async-start | bytes 3538944 | tf_op jit(solution)/shard_map/all_to_all | solution.py:239
  301.3 139.8 %collective-permute-start.25 = (f32[24,36864]{1,0:T(8,128)}, f32[24,36864]{1,0:T(8,128)}, u32[]{:S(2)}, u32[]{:S(2)}) collective-permute-start(f32[24,36864]{1,0:T(8,128)} %backward_yz.7), channel_id=1, source_target_pairs={{0,8},{1,9},{64,72},{65,73},{128,136},{129,137},{192,200},{193,201... | collective-permute-start | bytes 10616840 | tf_op jit(solution)/shard_map/ppermute | solution.py:248
  360.0 81.1 %collective-permute-start.26 = (bf16[24,36864]{1,0:T(8,128)(2,1)S(1)}, bf16[24,36864]{1,0:T(8,128)(2,1)S(1)}, u32[]{:S(2)}, u32[]{:S(2)}) collective-permute-start(bf16[24,36864]{1,0:T(8,128)(2,1)S(1)} %convert_element_type.21), channel_id=1, source_target_pairs={{72,0},{9,1},{136,64},{73,65},{200,128},{137,129},{8,192},{201,193... | collective-permute-start | bytes 5308424 | tf_op jit(solution)/shard_map/ppermute | solution.py:248
  361.4 79.7 %collective-permute-start.27 = (bf16[24,36864]{1,0:T(8,128)(2,1)S(1)}, bf16[24,36864]{1,0:T(8,128)(2,1)S(1)}, u32[]{:S(2)}, u32[]{:S(2)}) collective-permute-start(bf16[24,36864]{1,0:T(8,128)(2,1)S(1)} %copy-done.40), channel_id=1, source_target_pairs={{8,8},{201,9},{72,72},{9,73},{136,136},{73,137},{200,200},{137,201... | collective-permute-start | bytes 5308424 | tf_op jit(solution)/shard_map/ppermute | solution.py:248
  (53 other events, 482.9 us)
